TPU v7x, 512 devices: a whole 4x8x8 slice. The times are simulated.
512 devices in a mesh: grp: 16 (over y, core), shard: 32 (over x, z).
Axes of the slice: x: 4, y: 8, z: 8, core: 2. Of those that a mesh axis runs over, the one named last changes fastest.
Arguments:
- table: float32 [32768, 64], P('shard'), may hold values from -6 to 6
- accum: float32 [32768, 64], P('shard'), may hold values from 0.1 to 10
- grad_values: float32 [65536, 64], P(('grp', 'shard')), may hold values from -6 to 6
- grad_rows: int32 [65536], P(('grp', 'shard')), may hold values from 0 to 1023
- grad_counts: int32 [16384], P(('grp', 'shard')), may hold values from 1 to 4
- bucket_ids: int32 [131072, 24, 2], P(('grp', 'shard')), may hold values from 0 to 32767, as said below
- bag_lengths: int32 [131072, 24], P(('grp', 'shard')), may hold values from 1 to 2
- w_hidden: bfloat16 [1536, 1024], P('shard'), may hold values from -0.15625 to 0.15625
- b_hidden: float32 [1024], replicated, may hold values from -3 to 3
- w_score: bfloat16 [1024], replicated, may hold values from -0.1875 to 0.1875
Outputs:
- table_out: float32 [32768, 64], P('shard')
- accum_out: float32 [32768, 64], P('shard')
- scores: float32 [131072], P(('grp', 'shard'))
Inputs may be any that keep to these rules, and one draw needn't show every extreme that they name: `bucket_ids`: counting all 24 x 2 id slots of a device's 256 requests, also those past a bag's length, and calling id // 1024 the owner: one owner gets exactly 768 of them, the same owner for every device of one group along grp, and every other owner's count differs from the others' by at most one.
All inputs are finite; a program needn't handle non-finite values.
Results may differ from a plain program's by a relative error of at most 0.0054.
Values may be sent and summed in bfloat16 or wider, within the bound.
No kernel may reach another device: no remote copies, remote signals or barrier semaphores. Data moves between devices by JAX's collectives and lax.ppermute only.
A program may use at most 64 MiB of HBM per device.

v0:
```python
import math

import jax
import jax.numpy as jnp
from jax import lax
from jax.sharding import PartitionSpec as P


def sum_into_rows(row_count, target_rows, slot_values):
    picks = (jnp.arange(row_count, dtype=jnp.int32)[:, None] == target_rows[None, :]).astype(
        jnp.float32
    )
    return jnp.dot(
        picks, slot_values, precision=lax.Precision.HIGHEST, preferred_element_type=jnp.float32
    )


def build_requests(owner_pick, within, local_rows, capacity):
    owner_total = owner_pick.shape[1]
    within_pick = (within[:, None] == jnp.arange(capacity, dtype=jnp.int32)[None, :]).astype(
        jnp.bfloat16
    )
    low_part = (local_rows % 256).astype(jnp.float32)
    high_part = (local_rows // 256).astype(jnp.float32)
    left_side = jnp.concatenate(
        [owner_pick * low_part[:, None], owner_pick * high_part[:, None]], axis=1
    ).astype(jnp.bfloat16)
    packed = jnp.einsum("sk,sc->kc", left_side, within_pick, preferred_element_type=jnp.float32)
    return (packed[owner_total:] * 256.0 + packed[:owner_total]).astype(jnp.int32)


def per_device(
    table,
    accum,
    grad_values,
    grad_rows,
    grad_counts,
    bucket_ids,
    bag_lengths,
    w_hidden,
    b_hidden,
    w_score,
):
    shard_count = lax.axis_size("shard")
    rows_here, row_width = table.shape
    slot_rows = grad_rows.shape[0] // shard_count
    live_rows = jnp.arange(slot_rows, dtype=jnp.int32)[None, :] < grad_counts[:, None]
    grad_slots = jnp.where(
        live_rows[:, :, None], grad_values.reshape(shard_count, slot_rows, row_width), 0.0
    )
    targets = grad_rows.reshape(shard_count, slot_rows)
    got_values, got_rows = (
        lax.all_to_all(grad_slots, "shard", split_axis=0, concat_axis=0, tiled=True),
        lax.all_to_all(targets, "shard", split_axis=0, concat_axis=0, tiled=True),
    )
    owned_sum = sum_into_rows(rows_here, got_rows.reshape(-1), got_values.reshape(-1, row_width))
    grad_sum = lax.psum(owned_sum, "grp")
    accum_out = accum + grad_sum * grad_sum
    table_out = table - 0.5 * grad_sum * lax.rsqrt(accum_out)
    serving_rows = table_out.astype(jnp.bfloat16)
    request_count, vocab_count, bag_size = bucket_ids.shape
    flat_ids = bucket_ids.reshape(-1)
    slot_count = flat_ids.shape[0]
    capacity = 2 * slot_count // shard_count
    owners = flat_ids // rows_here
    local_rows = flat_ids % rows_here
    owner_iota = jnp.arange(shard_count, dtype=jnp.int32)
    block_len = math.gcd(slot_count, 256)
    block_total = slot_count // block_len
    owner_hot = (
        owners.reshape(block_total, block_len)[:, :, None] == owner_iota[None, None, :]
    ).astype(jnp.bfloat16)
    position = jnp.arange(block_len, dtype=jnp.int32)
    lower_ones = (position[:, None] >= position[None, :]).astype(jnp.bfloat16)
    inclusive = jnp.einsum("ij,bjk->bik", lower_ones, owner_hot, preferred_element_type=jnp.float32)
    owner_float = owner_hot.astype(jnp.float32)
    block_sums = jnp.sum(owner_float, axis=1)
    block_offsets = jnp.cumsum(block_sums, axis=0) - block_sums
    ranks = inclusive + block_offsets[:, None, :]
    within = (jnp.sum(owner_float * ranks, axis=2) - 1.0).reshape(-1).astype(jnp.int32)
    owner_pick = owner_float.reshape(slot_count, shard_count)
    placed = owners * capacity + within
    requested = build_requests(owner_pick, within, local_rows, capacity)
    fetched = serving_rows[
        lax.all_to_all(requested, "shard", split_axis=0, concat_axis=0, tiled=True)
    ]
    returned = lax.all_to_all(fetched, "shard", split_axis=0, concat_axis=0, tiled=True)
    own_rows = returned.reshape(shard_count * capacity, row_width)[placed]
    own_rows = own_rows.reshape(request_count, vocab_count, bag_size, row_width)
    in_bag = jnp.arange(bag_size, dtype=jnp.int32)[None, None, :] < bag_lengths[:, :, None]
    pooled = jnp.sum(jnp.where(in_bag[..., None], own_rows.astype(jnp.float32), 0.0), axis=2)
    pooled = pooled.astype(jnp.bfloat16).reshape(request_count, vocab_count * row_width)
    hidden_pre = jnp.dot(
        pooled,
        lax.all_gather(w_hidden, "shard", axis=0, tiled=True),
        preferred_element_type=jnp.float32,
    )
    hidden = jax.nn.silu(hidden_pre + b_hidden).astype(jnp.bfloat16)
    scores = jnp.dot(hidden, w_score, preferred_element_type=jnp.float32)
    return (table_out, accum_out, scores)


def solution(mesh):
    return jax.shard_map(
        per_device,
        mesh=mesh,
        in_specs=(
            P("shard", None),
            P("shard", None),
            P(("grp", "shard"), None),
            P(("grp", "shard")),
            P(("grp", "shard")),
            P(("grp", "shard"), None, None),
            P(("grp", "shard"), None),
            P("shard", None),
            P(),
            P(),
        ),
        out_specs=(P("shard", None), P("shard", None), P(("grp", "shard"))),
        check_vma=False,
    )
```

profile of v0, /device:TPU:1, one launch (start us, length us, event | category | flops | bytes accessed | tf_op | source)
XLA Modules:
  0.0 441.6 jit_solution(10169167343859944870)
XLA Ops:
  8.0 1.4 all_to_all.20
  9.4 13.7 %all-to-all-start = ((s32[32,1,4]{2,1,0:T(1,128)}), s32[32,1,4]{2,1,0:T(1,128)S(1)}, u32[]{:S(2)}, u32[]{:S(2)}) async-start(s32[32,1,4]{2,1,0:T(1,128)} %bitcast), calls=%async_computation | async-start | bytes 32768 | tf_op jit(solution)/shard_map/all_to_all | solution.py:54
  23.1 1.8 copy.46
  24.9 2.1 reshape.301
  27.0 0.0 copy-start.1
  27.0 2.1 reshape.302
  29.2 0.1 fusion.22
  29.3 0.3 convert_reduce_fusion
  29.6 0.1 reduce_window_sum.11
  29.7 0.7 fusion.5
  30.3 0.6 convert_bitcast_fusion
  31.0 0.0 copy-done.1
  31.0 0.1 copy.44
  31.1 0.0 copy-done.4
  31.1 0.1 iota_compare_fusion.11
  31.2 0.3 fusion.3
  31.5 7.7 %fusion = f32[64,768]{1,0:T(8,128)S(1)} fusion(s32[12288]{0:T(1024)S(1)} %bitcast.41, bf16[12288,32]{0,1:T(8,128)(2,1)S(1)} %get-tuple-element.9, bf16[12288,32]{0,1:T(8,128)(2,1)S(1)} %get-tuple-element.8), kind=kOutput, calls=%fused_computation.3 | convolution fusion | flops 1220542464 | bytes 1818624 | tf_op jit(solution)/shard_map/sk,sc->kc/dot_general | solution.py:28
  39.1 0.1 broadcast_select_fusion
  39.2 0.7 reshape.335
  40.0 0.0 all-to-all-done
  40.0 9.2 %all-to-all-start.1 = ((f32[32,1,256]{2,1,0:T(1,128)}), f32[32,1,256]{2,1,0:T(1,128)S(1)}, u32[]{:S(2)}, u32[]{:S(2)}) async-start(f32[32,1,256]{2,1,0:T(1,128)} %reshape.335), calls=%async_computation.1 | async-start | bytes 65536 | tf_op jit(solution)/shard_map/all_to_all | solution.py:53
  49.2 0.7 copy.48
  50.0 0.5 broadcast.276
  50.5 0.7 reduce.3
  51.2 0.1 eq.52
  51.3 6.7 %all-to-all-done.1 = f32[32,1,256]{2,1,0:T(1,128)S(1)} async-done(((f32[32,1,256]{2,1,0:T(1,128)}), f32[32,1,256]{2,1,0:T(1,128)S(1)}, u32[]{:S(2)}, u32[]{:S(2)}) %all-to-all-start.1) | async-done | bytes 32800 | tf_op jit(solution)/shard_map/all_to_all | solution.py:53
  58.0 3.9 all-to-all-start.2
  61.8 0.0 all-reduce.2.cloned.1.call-start
  61.9 0.5 broadcast.277
  62.4 0.7 reduce.4
  63.1 0.1 reshape.336
  63.2 1.1 fusion.16
  64.3 0.0 all-reduce.2.cloned.1.call-update
  64.4 6.5 %all-to-all-done.2 = s32[32,1,768]{2,1,0:T(1,128)S(1)} async-done(((s32[32,1,768]{2,1,0:T(1,128)}), s32[32,1,768]{2,1,0:T(1,128)S(1)}, u32[]{:S(2)}, u32[]{:S(2)}) %all-to-all-start.2) | async-done | bytes 98336 | tf_op jit(solution)/shard_map/all_to_all | solution.py:85
  70.8 0.1 compare_select_fusion
  71.0 0.7 broadcast_clamp_fusion
  71.6 111.0 %all-reduce.2.cloned.1.call-done = f32[1024,64]{0,1:T(8,128)} async-done(((f32[1024,64]{0,1:T(8,128)}), f32[1024,64]{0,1:T(8,128)}) %all-reduce.2.cloned.1.call-update) | async-done | bytes 262160 | tf_op jit(solution)/shard_map/psum | solution.py:57
  182.6 2.0 fusion.32
  184.6 0.2 copy.49
  184.8 93.6 %gather_fusion = bf16[24576,64]{1,0:T(8,128)(2,1)} fusion(bf16[1024,64]{1,0:T(8,128)(2,1)S(1)} %copy.49, s32[24576]{0:T(1024)} %broadcast_clamp_fusion), kind=kCustom, calls=%fused_computation | custom fusion | bytes 6389760 | tf_op jit(solution)/shard_map/gather | solution.py:84
  278.4 6.8 %copy.50 = bf16[32,768,64]{1,2,0:T(8,128)(2,1)} copy(bf16[32,768,64]{2,1,0:T(8,128)(2,1)} %bitcast.33) | data formatting | bytes 6291456 | tf_op jit(solution)/shard_map/gather | solution.py:84
  285.2 10.0 %all-to-all-start.3 = ((bf16[32,768,64]{1,2,0:T(8,128)(2,1)}), bf16[32,768,64]{1,2,0:T(8,128)(2,1)}, u32[]{:S(2)}, u32[]{:S(2)}) async-start(bf16[32,768,64]{1,2,0:T(8,128)(2,1)} %copy.50), calls=%async_computation.3 | async-start | bytes 6291456 | tf_op jit(solution)/shard_map/all_to_all | solution.py:87
  295.2 0.0 copy-start
  295.3 0.0 copy-start.2
  295.3 0.0 copy-start.3
  295.3 0.0 all-gather.2.cloned.1.call-start
  295.3 0.5 all-gather.2.cloned.1.call-update
  295.9 2.2 reshape.304
  298.1 0.0 copy-done
  298.1 0.1 copy.55
  298.1 0.0 copy-done.2
  298.1 0.1 copy.45
  298.2 0.0 copy-done.3
  298.3 2.2 iota_compare_fusion.2
  300.5 0.3 compare_select_fusion.1
  300.8 69.0 %all-to-all-done.3 = bf16[32,768,64]{1,2,0:T(8,128)(2,1)} async-done(((bf16[32,768,64]{1,2,0:T(8,128)(2,1)}), bf16[32,768,64]{1,2,0:T(8,128)(2,1)}, u32[]{:S(2)}, u32[]{:S(2)}) %all-to-all-start.3) | async-done | bytes 3145760 | tf_op jit(solution)/shard_map/all_to_all | solution.py:87
  369.8 6.6 %copy.51 = bf16[32,768,64]{2,1,0:T(8,128)(2,1)} copy(bf16[32,768,64]{1,2,0:T(8,128)(2,1)} %all-to-all-done.3) | data formatting | bytes 6291456 | tf_op jit(solution)/shard_map/all_to_all | solution.py:87
  376.4 36.4 %gather_fusion.1 = bf16[12288,64]{1,0:T(8,128)(2,1)S(1)} fusion(bf16[24576,64]{1,0:T(8,128)(2,1)} %bitcast.32, s32[12288]{0:T(1024)S(1)} %broadcast_clamp_fusion.1), kind=kCustom, calls=%fused_computation.1 | custom fusion | bytes 3194880 | tf_op jit(solution)/shard_map/gather | solution.py:88
  412.8 0.0 copy-start.5
  412.8 15.5 %fusion.2 = bf16[256,24,64]{2,1,0:T(8,128)(2,1)} fusion(bf16[256,24,2,64]{3,2,1,0:T(2,128)(2,1)S(1)} %bitcast.34, pred[256,24,2]{2,1,0:T(8,128)(4,1)} %iota_compare_fusion.2), kind=kLoop, calls=%fused_computation.6 | loop fusion | flops 1966080 | bytes 2371584 | tf_op jit(solution)/shard_map/reduce_sum | solution.py:91
  428.4 2.0 copy.53
  430.4 0.0 all-gather.2.cloned.1.call-done
  430.4 0.0 copy-done.5
  430.4 3.7 fusion.12
  (7 shorter events, 0.1 us)
Async XLA Ops:
  9.4 30.6 %all-to-all-start = ((s32[32,1,4]{2,1,0:T(1,128)}), s32[32,1,4]{2,1,0:T(1,128)S(1)}, u32[]{:S(2)}, u32[]{:S(2)}) async-start(s32[32,1,4]{2,1,0:T(1,128)} %bitcast), calls=%async_computation | async-start | bytes 32768 | tf_op jit(solution)/shard_map/all_to_all | solution.py:54
  27.0 4.0 copy-start.1
  27.0 4.1 copy-start.4
  40.0 18.0 %all-to-all-start.1 = ((f32[32,1,256]{2,1,0:T(1,128)}), f32[32,1,256]{2,1,0:T(1,128)S(1)}, u32[]{:S(2)}, u32[]{:S(2)}) async-start(f32[32,1,256]{2,1,0:T(1,128)} %reshape.335), calls=%async_computation.1 | async-start | bytes 65536 | tf_op jit(solution)/shard_map/all_to_all | solution.py:53
  58.0 12.9 %all-to-all-start.2 = ((s32[32,1,768]{2,1,0:T(1,128)}), s32[32,1,768]{2,1,0:T(1,128)S(1)}, u32[]{:S(2)}, u32[]{:S(2)}) async-start(s32[32,1,768]{2,1,0:T(1,128)} %copy.48), calls=%async_computation.2 | async-start | bytes 196608 | tf_op jit(solution)/shard_map/all_to_all | solution.py:85
  61.8 120.8 %all-reduce.2.cloned.1.call-start = ((), (), s32[]{:S(2)}) async-start(), calls=%async_computation.4 | async-start | bytes 524288 | tf_op jit(solution)/shard_map/psum | solution.py:57
  285.2 84.6 %all-to-all-start.3 = ((bf16[32,768,64]{1,2,0:T(8,128)(2,1)}), bf16[32,768,64]{1,2,0:T(8,128)(2,1)}, u32[]{:S(2)}, u32[]{:S(2)}) async-start(bf16[32,768,64]{1,2,0:T(8,128)(2,1)} %copy.50), calls=%async_computation.3 | async-start | bytes 6291456 | tf_op jit(solution)/shard_map/all_to_all | solution.py:87
  295.2 2.8 copy-start
  295.3 2.9 copy-start.2
  295.3 3.0 copy-start.3
  295.3 135.1 %all-gather.2.cloned.1.call-start = ((), (), s32[]{:S(2)}) async-start(), calls=%async_computation.5 | async-start | bytes 3244032 | tf_op jit(solution)/shard_map/all_gather | solution.py:95
  412.8 17.6 %copy-start.5 = (f32[1024]{0:T(1024)S(1)}, f32[1024]{0:T(1024)}, u32[]{:S(2)}) copy-start(f32[1024]{0:T(1024)} %param.18) | copy-start | bytes 12292
Sparse Core Ops, SparseCore 0:
  65.5 117.0 all-reduce.1
Sparse Core Ops, SparseCore 1:
  299.4 93.2 all-gather.1
where the time goes:
time: 447 us; the launch traced here: 442 us
  waiting for transfers between devices  194 us (43%)
  local copies, waits for them, and re-layouts  158 us (35%)
  starting transfers between devices  36.9 us (8%)
  other arithmetic  23.7 us (5%)
  between operations  15.8 us (4%)
  matrix products  13.2 us (3%)
    psum x1, waiting for transfers between devices, per_device(): grad_sum = lax.psum(owned_sum, 'grp')  111 us
    gather x2, local copies, waits for them, and re-layouts, per_device(): serving_rows[lax.all_to_all(requested, 'shard', split_axis=0, concat_axis...  100 us
    all_to_all x1, waiting for transfers between devices, per_device(): lax.all_to_all(fetched, 'shard', split_axis=0, concat_axis=0, tiled=True)  69 us
    gather x1, local copies, waits for them, and re-layouts, per_device(): own_rows = returned.reshape(shard_count * capacity, row_width)[placed]  36.4 us
    reduce_sum x1, other arithmetic, per_device(): jnp.sum(jnp.where(in_bag[..., None], own_rows.astype(jnp.float32), 0.0),...  15.5 us
    all_to_all x1, starting transfers between devices, per_device(): lax.all_to_all(targets, 'shard', split_axis=0, concat_axis=0, tiled=True)  13.7 us
    all_to_all x1, starting transfers between devices, per_device(): lax.all_to_all(fetched, 'shard', split_axis=0, concat_axis=0, tiled=True)  10 us
    all_to_all x1, starting transfers between devices, per_device(): lax.all_to_all(grad_slots, 'shard', split_axis=0, concat_axis=0, tiled=True)  9.23 us
  transfers between devices with their start and end apart: 6, of which 4 were waited for; matrix products, arithmetic and copies ran while one was open for 20% of the time, Pallas kernels for 0%

commit v1 on v0

v1 whole, which is shorter than its diff:
```python
import functools

import jax
import jax.numpy as jnp
from jax import lax
from jax.experimental import pallas as pl
from jax.experimental.pallas import tpu as pltpu
from jax.sharding import Mesh
from jax.sharding import PartitionSpec as P

BF = jnp.bfloat16
F32 = jnp.float32
VMEM = pl.BlockSpec(memory_space=pltpu.VMEM)
SMEM = pl.BlockSpec(memory_space=pltpu.SMEM)
HALF = 8192
PARAMS = pltpu.CompilerParams(vmem_limit_bytes=56 * 2**20)


def message_kernel(values_t, rows, counts, out):
    owners, slots = counts.shape[1], rows.shape[1]
    per_owner = slots // owners
    spread = (
        lax.broadcasted_iota(jnp.int32, (owners, slots), 0)
        == lax.broadcasted_iota(jnp.int32, (owners, slots), 1) // per_owner
    ).astype(BF)
    many = jnp.broadcast_to(counts[...].astype(F32), (8, owners)).astype(BF)
    live = jnp.dot(many, spread, preferred_element_type=F32)
    place = lax.broadcasted_iota(jnp.int32, (1, slots), 1) % per_owner
    target = jnp.where(place < live[:1].astype(jnp.int32), rows[...], -64)
    high = jnp.broadcast_to(target >> 5, (64, slots)).astype(F32)
    low = jnp.broadcast_to(target & 31, (64, slots)).astype(F32)
    first = lax.broadcasted_iota(jnp.int32, (64, slots), 0) == 0
    digits = jnp.where(first, high, low)
    out[...] = jnp.concatenate([values_t[...], digits], axis=0).T.astype(BF)


def update_kernel(core, message, table_t, accum_t, table_out, accum_out, block):
    rows = table_t.shape[1]
    total = jnp.zeros((128, rows), F32)
    step = 512
    for start in range(0, message.shape[0], step):
        part = message[start : start + step]
        target = (part[:, 64:65].astype(F32) * 32.0 + part[:, 65:66].astype(F32)).astype(jnp.int32)
        picks = (target == lax.broadcasted_iota(jnp.int32, (step, rows), 1)).astype(F32).astype(BF)
        total += lax.dot_general(part, picks, (((0,), (0,)), ((), ())), preferred_element_type=F32)
    grad = total[:64]
    accum_new = accum_t[...] + grad * grad
    table_new = table_t[...] - 0.5 * grad * lax.rsqrt(accum_new)
    accum_out[...] = accum_new
    table_out[...] = table_new
    stacked = jnp.concatenate([table_new[:, : rows // 2], table_new[:, rows // 2 :]], axis=0)
    mine = jnp.where(core[0] == 0, stacked[:, : rows // 4], stacked[:, rows // 4 :])
    serving = mine.T.astype(BF)
    for i in range(block.shape[0]):
        block[i] = serving


def score_kernel(ids, own, other, weights, bias, head, out, rows, pooled):
    step = 256

    def spread(i, carry):
        start = pl.multiple_of(i * step, step)
        for k, half in enumerate((own, other)):
            value = half[pl.ds(start, step), :].astype(F32)
            rows[pl.ds(start + k * HALF, step), :] = value
            rows[pl.ds(start + (2 + k) * HALF, step), :] = pltpu.roll(value, 64, 1)
        return carry

    lax.fori_loop(0, HALF // step, spread, 0)
    rows[pl.ds(4 * HALF, 8), :] = jnp.zeros((8, 128), F32)
    left = lax.broadcasted_iota(jnp.int32, (1, 128), 1) < 64
    vocabs = ids.shape[0]

    def look_up(r, carry):
        for j in range(vocabs // 2):
            one = rows[pl.ds(ids[2 * j, 0, r], 1), :] + rows[pl.ds(ids[2 * j, 1, r], 1), :]
            two = rows[pl.ds(ids[2 * j + 1, 0, r], 1), :] + rows[pl.ds(ids[2 * j + 1, 1, r], 1), :]
            pooled[j, pl.ds(r, 1), :] = jnp.where(left, one, two)
        return carry

    lax.fori_loop(0, pooled.shape[1], look_up, 0)
    features = jnp.concatenate([pooled[j].astype(BF) for j in range(vocabs // 2)], axis=1)
    unit = jnp.dot(features, weights[...], preferred_element_type=F32) + bias[...]
    hidden = (unit / (1.0 + jnp.exp(-unit))).astype(BF)
    heads = jnp.broadcast_to(head[...].astype(F32), (8, head.shape[1])).astype(BF)
    out[...] = lax.dot_general(heads, hidden, (((1,), (1,)), ((), ())), preferred_element_type=F32)


def per_device(
    table,
    accum,
    grad_values,
    grad_rows,
    grad_counts,
    bucket_ids,
    bag_lengths,
    w_hidden,
    b_hidden,
    w_score,
):
    core = lax.axis_index("c")
    weights = lax.all_gather(w_hidden, ("x", "z"), axis=0, tiled=True)
    message = pl.pallas_call(
        message_kernel,
        out_shape=jax.ShapeDtypeStruct((128, 128), BF),
        in_specs=[VMEM] * 3,
        out_specs=VMEM,
        name="message",
    )(grad_values.T, grad_rows[None, :], grad_counts[None, :])
    got = lax.all_to_all(message.reshape(32, 4, 128), ("x", "z"), 0, 0, tiled=True)
    slots = lax.all_gather(got, ("y", "c"), axis=0, tiled=True).reshape(2048, 128)
    table_out, accum_out, block = pl.pallas_call(
        update_kernel,
        out_shape=(
            jax.ShapeDtypeStruct((64, 1024), F32),
            jax.ShapeDtypeStruct((64, 1024), F32),
            jax.ShapeDtypeStruct((8, 256, 128), BF),
        ),
        in_specs=[SMEM] + [VMEM] * 3,
        out_specs=(VMEM,) * 3,
        compiler_params=PARAMS,
        name="update",
    )(core[None], slots, table.T, accum.T)
    column = lax.all_to_all(block, "z", 0, 0, tiled=True).reshape(1, 2048, 128)
    own = lax.all_to_all(jnp.broadcast_to(column, (4, 2048, 128)), "x", 0, 0, tiled=True).reshape(HALF, 128)
    other = lax.ppermute(own, "c", [(0, 1), (1, 0)])

    ids = bucket_ids.transpose(1, 2, 0)
    vocab = lax.broadcasted_iota(jnp.int32, ids.shape, 0)
    turned = ((ids >> 9) ^ vocab) & 1
    away = ((ids >> 8) & 1) ^ core
    places = turned * (2 * HALF) + away * HALF + (ids >> 10) * 256 + (ids & 255)
    used = lax.broadcasted_iota(jnp.int32, ids.shape, 1) < bag_lengths.T[:, None, :]
    places = jnp.where(used, places, 4 * HALF)
    scores = pl.pallas_call(
        score_kernel,
        out_shape=jax.ShapeDtypeStruct((8, 256), F32),
        in_specs=[SMEM] + [VMEM] * 5,
        out_specs=VMEM,
        scratch_shapes=[pltpu.VMEM((4 * HALF + 8, 128), F32), pltpu.VMEM((12, 256, 128), F32)],
        compiler_params=PARAMS,
        name="score",
    )(places, own, other, weights, b_hidden[None, :], w_score[None, :])
    return (table_out.T, accum_out.T, scores[0])


def solution(mesh):
    shards = ("x", "z")
    every = ("y", "c", "x", "z")
    inner = Mesh(mesh.devices.reshape(8, 2, 4, 8), every)
    return jax.shard_map(
        per_device,
        mesh=inner,
        in_specs=(
            P(shards, None),
            P(shards, None),
            P(every, None),
            P(every),
            P(every),
            P(every, None, None),
            P(every, None),
            P(shards, None),
            P(),
            P(),
        ),
        out_specs=(P(shards, None), P(shards, None), P(every)),
        check_vma=False,
    )
```

time: 447 us -> 149 us (0.33); the launches traced: 442 us -> 148 us
  waiting for transfers between devices: 194 us -> 12 us
  local copies, waits for them, and re-layouts: 158 us -> 2.14 us
  blocking collectives: 0 us -> 75.5 us
  Pallas kernels: 0 us -> 26.4 us
  other arithmetic: 23.7 us -> 0.72 us
  starting transfers between devices: 36.9 us -> 17.5 us
  matrix products: 13.2 us -> 0 us
    gather x3 -> x0, local copies, waits for them, and re-layouts: 137 us -> none  [the longest x2 100 us: per_device(): serving_rows[lax.all_to_all(requested, 'shard', split_axis=0, concat_axis...]
    psum x1 -> x0, waiting for transfers between devices: 111 us -> none  [per_device(): grad_sum = lax.psum(owned_sum, 'grp')]
    all_to_all x4 -> x1, waiting for transfers between devices: 82.2 us -> 8.76 us  [per_device(): lax.all_to_all(message.reshape(32, 4, 128), ('x', 'z'), 0, 0, tiled=True)]
    all_to_all x0 -> x2, blocking collectives: none -> 53.1 us  [the longest x1 32.2 us: per_device(): lax.all_to_all(jnp.broadcast_to(column, (4, 2048, 128)), 'x', 0, 0, tiled...]
    pallas_call x0 -> x3, Pallas kernels: none -> 26.4 us  [the longest x1 21.2 us: per_device(): pl.pallas_call(score_kernel, out_shape=jax.ShapeDtypeStruct((8, 256), F32...]
    all_to_all x4 -> x1, starting transfers between devices: 36.8 us -> 13.7 us  [per_device(): lax.all_to_all(message.reshape(32, 4, 128), ('x', 'z'), 0, 0, tiled=True)]
    all_gather x0 -> x1, blocking collectives: none -> 22.3 us  [per_device(): lax.all_gather(got, ('y', 'c'), axis=0, tiled=True).reshape(2048, 128)]
    reduce_sum x2 -> x0, other arithmetic: 15.8 us -> none  [the longest x1 15.5 us: per_device(): jnp.sum(jnp.where(in_bag[..., None], own_rows.astype(jnp.float32), 0.0),...]
  transfers between devices with their start and end apart: 6 -> 3, of which waited for: 4 -> 2; matrix products, arithmetic and copies ran while one was open for 20% -> 1% of each run, Pallas kernels for 0% -> 3%
where the time goes in v1:
time: 149 us; the launch traced here: 148 us
  blocking collectives  75.5 us (51%)
  Pallas kernels  26.4 us (18%)
  starting transfers between devices  17.5 us (12%)
  between operations  14.1 us (9%)
  waiting for transfers between devices  12 us (8%)
  local copies, waits for them, and re-layouts  2.14 us (1%)
    all_to_all x1, blocking collectives, per_device(): lax.all_to_all(jnp.broadcast_to(column, (4, 2048, 128)), 'x', 0, 0, tiled...  32.2 us
    all_gather x1, blocking collectives, per_device(): lax.all_gather(got, ('y', 'c'), axis=0, tiled=True).reshape(2048, 128)  22.3 us
    pallas_call x1, Pallas kernels, per_device(): pl.pallas_call(score_kernel, out_shape=jax.ShapeDtypeStruct((8, 256), F32...  21.2 us
    all_to_all x1, blocking collectives, per_device(): column = lax.all_to_all(block, 'z', 0, 0, tiled=True).reshape(1, 2048, 128)  20.9 us
    all_to_all x1, starting transfers between devices, per_device(): lax.all_to_all(message.reshape(32, 4, 128), ('x', 'z'), 0, 0, tiled=True)  13.7 us
    all_to_all x1, waiting for transfers between devices, per_device(): lax.all_to_all(message.reshape(32, 4, 128), ('x', 'z'), 0, 0, tiled=True)  8.76 us
    ppermute x1, starting transfers between devices, per_device(): other = lax.ppermute(own, 'c', [(0, 1), (1, 0)])  3.76 us
    pallas_call x1, Pallas kernels, per_device(): pl.pallas_call(update_kernel, out_shape=(jax.ShapeDtypeStruct((64, 1024),...  3.54 us
  transfers between devices with their start and end apart: 3, of which 2 were waited for; matrix products, arithmetic and copies ran while one was open for 1% of the time, Pallas kernels for 3%

profile of v1, /device:TPU:1, one launch (start us, length us, event | category | flops | bytes accessed | tf_op | source)
XLA Modules:
  0.0 148.3 jit_solution(8957265796817876861)
XLA Ops:
  7.2 0.0 all-gather.2.cloned.1.call-start
  7.2 0.7 all-gather.2.cloned.1.call-update
  7.9 1.6 %message.1 = bf16[128,128]{1,0:T(8,128)(2,1)} custom-call(f32[64,128]{1,0:T(8,128)} %bitcast.42, s32[1,128]{1,0:T(1,128)} %bitcast.46, s32[1,32]{1,0:T(1,128)} %bitcast.47), custom_call_target="tpu_custom_call" | custom-call | tf_op jit(solution)/shard_map/message/pallas_call | solution.py:103
  9.5 13.7 %all-to-all-start = ((bf16[32,4,128]{2,1,0:T(4,128)(2,1)}), bf16[32,4,128]{2,1,0:T(4,128)(2,1)S(1)}, u32[]{:S(2)}, u32[]{:S(2)}) async-start(bf16[32,4,128]{2,1,0:T(4,128)(2,1)} %bitcast.41), calls=%async_computation | async-start | bytes 65536 | tf_op jit(solution)/shard_map/all_to_all | solution.py:110
  23.2 8.8 %all-to-all-done = bf16[32,4,128]{2,1,0:T(4,128)(2,1)S(1)} async-done(((bf16[32,4,128]{2,1,0:T(4,128)(2,1)}), bf16[32,4,128]{2,1,0:T(4,128)(2,1)S(1)}, u32[]{:S(2)}, u32[]{:S(2)}) %all-to-all-start) | async-done | bytes 32800 | tf_op jit(solution)/shard_map/all_to_all | solution.py:110
  32.0 22.3 %all_gather.6 = bf16[512,4,128]{2,1,0:T(4,128)(2,1)} all-gather(bf16[32,4,128]{2,1,0:T(4,128)(2,1)S(1)} %all-to-all-done), channel_id=1, replica_groups=mesh['y'=8,'c'=2,'x'=4,'z'=8] {'y','c'}, dimensions={0}, use_global_device_ids=true | all-gather | bytes 557056 | tf_op jit(solution)/shard_map/all_gather | solution.py:111
  54.3 3.5 %update.1 = (f32[64,1024]{1,0:T(8,128)}, f32[64,1024]{1,0:T(8,128)}, bf16[8,256,128]{2,1,0:T(8,128)(2,1)}) custom-call(s32[1]{0:T(128)} %bitcast.core, bf16[2048,128]{1,0:T(8,128)(2,1)} %bitcast.38, f32[64,1024]{1,0:T(8,128)} %bitcast.39, f32[64,1024]{1,0:T(8,128)} %bitcast.40), custom_call_target="tpu_custom_call" | custom-call | tf_op jit(solution)/shard_map/update/pallas_call | solution.py:112
  57.9 20.9 %all_to_all.15 = bf16[8,256,128]{2,1,0:T(8,128)(2,1)S(1)} all-to-all(bf16[8,256,128]{2,1,0:T(8,128)(2,1)} %get-tuple-element.8), channel_id=1, replica_groups=mesh['y'=8,'c'=2,'x'=4,'z'=8] {'z'}, dimensions={0} | all-to-all | bytes 1048576 | tf_op jit(solution)/shard_map/all_to_all | solution.py:124
  78.8 0.3 broadcast_in_dim.32
  79.0 0.0 copy-start.3
  79.0 0.0 copy-start.1
  79.1 0.0 copy-start.2
  79.1 32.2 %all_to_all.16 = bf16[4,2048,128]{2,1,0:T(8,128)(2,1)S(1)} all-to-all(bf16[4,2048,128]{2,1,0:T(8,128)(2,1)S(1)} %broadcast_in_dim.32), channel_id=1, replica_groups=mesh['y'=8,'c'=2,'x'=4,'z'=8] {'x'}, dimensions={0} | all-to-all | bytes 4194304 | tf_op jit(solution)/shard_map/all_to_all | solution.py:125
  111.3 0.0 copy-start
  111.3 3.8 %collective-permute-start = (bf16[8192,128]{1,0:T(8,128)(2,1)S(1)}, bf16[8192,128]{1,0:T(8,128)(2,1)}, u32[]{:S(2)}, u32[]{:S(2)}) collective-permute-start(bf16[8192,128]{1,0:T(8,128)(2,1)S(1)} %bitcast.35), channel_id=1, source_target_pairs={{0,32},{32,0},{1,33},{33,1},{2,34},{34,2},{3,35},{35,3},{4,36},{36... | collective-permute-start | bytes 6291464 | tf_op jit(solution)/shard_map/ppermute | solution.py:126
  115.1 0.0 copy-done.3
  115.1 0.6 broadcast_in_dim.34.head
  115.7 0.0 copy-done.1
  115.7 0.0 copy-done.2
  115.7 0.7 compare_select_fusion.ids
  116.4 2.6 %collective-permute-done.other = bf16[8192,128]{1,0:T(8,128)(2,1)} collective-permute-done((bf16[8192,128]{1,0:T(8,128)(2,1)S(1)}, bf16[8192,128]{1,0:T(8,128)(2,1)}, u32[]{:S(2)}, u32[]{:S(2)}) %collective-permute-start) | collective-permute-done | bytes 2097184 | tf_op jit(solution)/shard_map/ppermute | solution.py:126
  119.0 0.0 all-gather.2.cloned.1.call-done.weights
  119.0 0.0 copy-done
  119.0 21.2 %score.1 = f32[8,256]{1,0:T(8,128)} custom-call(s32[24,2,256]{2,1,0:T(2,128)} %compare_select_fusion.ids, bf16[8192,128]{1,0:T(8,128)(2,1)} %bitcast.36, bf16[8192,128]{1,0:T(8,128)(2,1)} %collective-permute-done.other, bf16[1536,1024]{1,0:T(8,128)(2,1)} %all-gather.2.cloned.1.call-done.weights, f32[1,1024]{1,0:T(1,128)} %bitcast.44, ...), custom_call_target="tpu_custom_call" | custom-call | tf_op jit(solution)/shard_map/score/pallas_call | solution.py:135
  140.2 1.3 slice.4
Async XLA Ops:
  7.2 111.8 %all-gather.2.cloned.1.call-start = ((), (), s32[]{:S(2)}) async-start(), calls=%async_computation.3 | async-start | bytes 3244032 | tf_op jit(solution)/shard_map/all_gather | solution.py:102
  9.5 22.5 %all-to-all-start = ((bf16[32,4,128]{2,1,0:T(4,128)(2,1)}), bf16[32,4,128]{2,1,0:T(4,128)(2,1)S(1)}, u32[]{:S(2)}, u32[]{:S(2)}) async-start(bf16[32,4,128]{2,1,0:T(4,128)(2,1)} %bitcast.41), calls=%async_computation | async-start | bytes 65536 | tf_op jit(solution)/shard_map/all_to_all | solution.py:110
  79.0 36.0 %copy-start.3 = (bf16[1024]{0:T(1024)(128)(2,1)S(1)}, bf16[1024]{0:T(1024)(128)(2,1)}, u32[]{:S(2)}) copy-start(bf16[1024]{0:T(1024)(128)(2,1)} %param.19) | copy-start | bytes 6148
  79.0 36.6 %copy-start.1 = (s32[256,24,2]{0,2,1:T(2,128)S(1)}, s32[256,24,2]{0,2,1:T(2,128)}, u32[]{:S(2)}) copy-start(s32[256,24,2]{0,2,1:T(2,128)} %param.15) | copy-start | bytes 147460
  79.1 36.6 %copy-start.2 = (s32[256,24]{0,1:T(8,128)S(1)}, s32[256,24]{0,1:T(8,128)}, u32[]{:S(2)}) copy-start(s32[256,24]{0,1:T(8,128)} %param.16) | copy-start | bytes 73732
  111.3 7.7 %copy-start = (bf16[4,2048,128]{2,1,0:T(8,128)(2,1)}, bf16[4,2048,128]{2,1,0:T(8,128)(2,1)S(1)}, u32[]{:S(2)}) copy-start(bf16[4,2048,128]{2,1,0:T(8,128)(2,1)S(1)} %all_to_all.16) | copy-start | bytes 6291460
  111.3 7.7 %collective-permute-start = (bf16[8192,128]{1,0:T(8,128)(2,1)S(1)}, bf16[8192,128]{1,0:T(8,128)(2,1)}, u32[]{:S(2)}, u32[]{:S(2)}) collective-permute-start(bf16[8192,128]{1,0:T(8,128)(2,1)S(1)} %bitcast.35), channel_id=1, source_target_pairs={{0,32},{32,0},{1,33},{33,1},{2,34},{34,2},{3,35},{35,3},{4,36},{36... | collective-permute-start | bytes 6291464 | tf_op jit(solution)/shard_map/ppermute | solution.py:126
Sparse Core Ops, SparseCore 0:
  11.2 97.4 all-gather.1

commit v2 on v1

--- a/solution.py
+++ b/solution.py
@@ -1,5 +1,3 @@
-import functools
-
 import jax
 import jax.numpy as jnp
 from jax import lax
@@ -11,6 +9,7 @@
 BF = jnp.bfloat16
 F32 = jnp.float32
 VMEM = pl.BlockSpec(memory_space=pltpu.VMEM)
+HBM = pl.BlockSpec(memory_space=pltpu.HBM)
 SMEM = pl.BlockSpec(memory_space=pltpu.SMEM)
 HALF = 8192
 PARAMS = pltpu.CompilerParams(vmem_limit_bytes=56 * 2**20)
@@ -55,35 +54,50 @@
         block[i] = serving
 
 
-def score_kernel(ids, own, other, weights, bias, head, out, rows, pooled):
-    step = 256
+def score_kernel(ids_in, own, other, weights_in, bias, head, out, ids, rows, pooled, staged, weights, table_sems, id_sem, weight_sem):
+    step = 2048
+    id_copy = pltpu.make_async_copy(ids_in, ids, id_sem)
+    id_copy.start()
+    copies = []
+    for k, half in enumerate((own, other)):
+        for start in range(0, HALF, step):
+            copies.append(
+                pltpu.make_async_copy(
+                    half.at[pl.ds(start, step)],
+                    staged.at[pl.ds(k * HALF + start, step)],
+                    table_sems.at[len(copies)],
+                )
+            )
+            copies[-1].start()
+    weight_copy = pltpu.make_async_copy(weights_in, weights, weight_sem)
+    weight_copy.start()
+    for i, copy in enumerate(copies):
+        copy.wait()
+        value = staged[i * step : (i + 1) * step].astype(F32)
+        rows[i * step : (i + 1) * step] = value
+        rows[2 * HALF + i * step : 2 * HALF + (i + 1) * step] = pltpu.roll(value, 64, 1)
+    rows[4 * HALF : 4 * HALF + 8] = jnp.zeros((8, 128), F32)
+    left = lax.broadcasted_iota(jnp.int32, (1, 128), 1) < 64
+    pairs, requests, _ = pooled.shape
+    id_copy.wait()
 
-    def spread(i, carry):
-        start = pl.multiple_of(i * step, step)
-        for k, half in enumerate((own, other)):
-            value = half[pl.ds(start, step), :].astype(F32)
-            rows[pl.ds(start + k * HALF, step), :] = value
-            rows[pl.ds(start + (2 + k) * HALF, step), :] = pltpu.roll(value, 64, 1)
+    def bag(vocab, r):
+        at = 2 * vocab * requests + r
+        return rows[pl.ds(ids[at], 1), :] + rows[pl.ds(ids[at + requests], 1), :]
+
+    def look_up(r, carry):
+        for j in range(pairs):
+            pooled[j, pl.ds(r, 1), :] = jnp.where(left, bag(2 * j, r), bag(2 * j + 1, r))
         return carry
 
-    lax.fori_loop(0, HALF // step, spread, 0)
-    rows[pl.ds(4 * HALF, 8), :] = jnp.zeros((8, 128), F32)
-    left = lax.broadcasted_iota(jnp.int32, (1, 128), 1) < 64
-    vocabs = ids.shape[0]
-
-    def look_up(r, carry):
-        for j in range(vocabs // 2):
-            one = rows[pl.ds(ids[2 * j, 0, r], 1), :] + rows[pl.ds(ids[2 * j, 1, r], 1), :]
-            two = rows[pl.ds(ids[2 * j + 1, 0, r], 1), :] + rows[pl.ds(ids[2 * j + 1, 1, r], 1), :]
-            pooled[j, pl.ds(r, 1), :] = jnp.where(left, one, two)
-        return carry
-
-    lax.fori_loop(0, pooled.shape[1], look_up, 0)
-    features = jnp.concatenate([pooled[j].astype(BF) for j in range(vocabs // 2)], axis=1)
+    lax.fori_loop(0, requests, look_up, 0, unroll=2)
+    features = jnp.concatenate([pooled[j].astype(BF) for j in range(pairs)], axis=1)
+    weight_copy.wait()
     unit = jnp.dot(features, weights[...], preferred_element_type=F32) + bias[...]
     hidden = (unit / (1.0 + jnp.exp(-unit))).astype(BF)
     heads = jnp.broadcast_to(head[...].astype(F32), (8, head.shape[1])).astype(BF)
-    out[...] = lax.dot_general(heads, hidden, (((1,), (1,)), ((), ())), preferred_element_type=F32)
+    scores = lax.dot_general(heads, hidden, (((1,), (1,)), ((), ())), preferred_element_type=F32)
+    out[...] = scores[0]
 
 
 def per_device(
@@ -134,14 +148,23 @@
     places = jnp.where(used, places, 4 * HALF)
     scores = pl.pallas_call(
         score_kernel,
-        out_shape=jax.ShapeDtypeStruct((8, 256), F32),
-        in_specs=[SMEM] + [VMEM] * 5,
+        out_shape=jax.ShapeDtypeStruct((256,), F32),
+        in_specs=[HBM] * 4 + [VMEM] * 2,
         out_specs=VMEM,
-        scratch_shapes=[pltpu.VMEM((4 * HALF + 8, 128), F32), pltpu.VMEM((12, 256, 128), F32)],
+        scratch_shapes=[
+            pltpu.SMEM((12288,), jnp.int32),
+            pltpu.VMEM((4 * HALF + 8, 128), F32),
+            pltpu.VMEM((12, 256, 128), F32),
+            pltpu.VMEM((2 * HALF, 128), BF),
+            pltpu.VMEM((1536, 1024), BF),
+            pltpu.SemaphoreType.DMA((8,)),
+            pltpu.SemaphoreType.DMA,
+            pltpu.SemaphoreType.DMA,
+        ],
         compiler_params=PARAMS,
         name="score",
-    )(places, own, other, weights, b_hidden[None, :], w_score[None, :])
-    return (table_out.T, accum_out.T, scores[0])
+    )(places.reshape(-1), own, other, weights, b_hidden[None, :], w_score[None, :])
+    return (table_out.T, accum_out.T, scores)
 
 
 def solution(mesh):

time: 149 us -> 142 us (0.953)
  Pallas kernels: 26.4 us -> 21.1 us
    pallas_call x1, Pallas kernels: 21.2 us -> 15.9 us  [per_device(): pl.pallas_call(score_kernel, out_shape=jax.ShapeDtypeStruct((256,), F32),...]
  transfers between devices with their start and end apart: 3 -> 3, of which waited for: 2 -> 2; matrix products, arithmetic and copies ran while one was open for 1% -> 1% of each run, Pallas kernels for 3% -> 4%
where the time goes in v2:
time: 142 us
  blocking collectives  75.5 us (53%)
  Pallas kernels  21.1 us (15%)
  starting transfers between devices  17.5 us (12%)
  between operations  14.1 us (10%)
  waiting for transfers between devices  12 us (8%)
  local copies, waits for them, and re-layouts  1.53 us (1%)
    all_to_all x1, blocking collectives, per_device(): lax.all_to_all(jnp.broadcast_to(column, (4, 2048, 128)), 'x', 0, 0, tiled...  32.2 us
    all_gather x1, blocking collectives, per_device(): lax.all_gather(got, ('y', 'c'), axis=0, tiled=True).reshape(2048, 128)  22.3 us
    all_to_all x1, blocking collectives, per_device(): column = lax.all_to_all(block, 'z', 0, 0, tiled=True).reshape(1, 2048, 128)  20.9 us
    pallas_call x1, Pallas kernels, per_device(): pl.pallas_call(score_kernel, out_shape=jax.ShapeDtypeStruct((256,), F32),...  15.9 us
    all_to_all x1, starting transfers between devices, per_device(): lax.all_to_all(message.reshape(32, 4, 128), ('x', 'z'), 0, 0, tiled=True)  13.7 us
    all_to_all x1, waiting for transfers between devices, per_device(): lax.all_to_all(message.reshape(32, 4, 128), ('x', 'z'), 0, 0, tiled=True)  8.76 us
    ppermute x1, starting transfers between devices, per_device(): other = lax.ppermute(own, 'c', [(0, 1), (1, 0)])  3.76 us
    pallas_call x1, Pallas kernels, per_device(): pl.pallas_call(update_kernel, out_shape=(jax.ShapeDtypeStruct((64, 1024),...  3.54 us
  transfers between devices with their start and end apart: 3, of which 2 were waited for; matrix products, arithmetic and copies ran while one was open for 1% of the time, Pallas kernels for 4%

profile of v2, /device:TPU:1, one launch (start us, length us, event | category | flops | bytes accessed | tf_op | source)
XLA Modules:
  0.0 141.8 jit_solution(11528834305511224206)
XLA Ops:
  7.2 0.0 all-gather.2.cloned.1.call-start
  7.2 0.7 all-gather.2.cloned.1.call-update
  7.9 1.6 %message.1 = bf16[128,128]{1,0:T(8,128)(2,1)} custom-call(f32[64,128]{1,0:T(8,128)} %bitcast.45, s32[1,128]{1,0:T(1,128)} %bitcast.48, s32[1,32]{1,0:T(1,128)} %bitcast.49), custom_call_target="tpu_custom_call" | custom-call | tf_op jit(solution)/shard_map/message/pallas_call | solution.py:117
  9.5 13.7 %all-to-all-start = ((bf16[32,4,128]{2,1,0:T(4,128)(2,1)}), bf16[32,4,128]{2,1,0:T(4,128)(2,1)S(1)}, u32[]{:S(2)}, u32[]{:S(2)}) async-start(bf16[32,4,128]{2,1,0:T(4,128)(2,1)} %bitcast.44), calls=%async_computation | async-start | bytes 65536 | tf_op jit(solution)/shard_map/all_to_all | solution.py:124
  23.2 8.8 %all-to-all-done = bf16[32,4,128]{2,1,0:T(4,128)(2,1)S(1)} async-done(((bf16[32,4,128]{2,1,0:T(4,128)(2,1)}), bf16[32,4,128]{2,1,0:T(4,128)(2,1)S(1)}, u32[]{:S(2)}, u32[]{:S(2)}) %all-to-all-start) | async-done | bytes 32800 | tf_op jit(solution)/shard_map/all_to_all | solution.py:124
  32.0 22.3 %all_gather.6 = bf16[512,4,128]{2,1,0:T(4,128)(2,1)} all-gather(bf16[32,4,128]{2,1,0:T(4,128)(2,1)S(1)} %all-to-all-done), channel_id=1, replica_groups=mesh['y'=8,'c'=2,'x'=4,'z'=8] {'y','c'}, dimensions={0}, use_global_device_ids=true | all-gather | bytes 557056 | tf_op jit(solution)/shard_map/all_gather | solution.py:125
  54.3 3.5 %update.1 = (f32[64,1024]{1,0:T(8,128)}, f32[64,1024]{1,0:T(8,128)}, bf16[8,256,128]{2,1,0:T(8,128)(2,1)}) custom-call(s32[1]{0:T(128)} %bitcast.core, bf16[2048,128]{1,0:T(8,128)(2,1)} %bitcast.40, f32[64,1024]{1,0:T(8,128)} %bitcast.41, f32[64,1024]{1,0:T(8,128)} %bitcast.42), custom_call_target="tpu_custom_call" | custom-call | tf_op jit(solution)/shard_map/update/pallas_call | solution.py:126
  57.9 20.9 %all_to_all.15 = bf16[8,256,128]{2,1,0:T(8,128)(2,1)S(1)} all-to-all(bf16[8,256,128]{2,1,0:T(8,128)(2,1)} %get-tuple-element.8), channel_id=1, replica_groups=mesh['y'=8,'c'=2,'x'=4,'z'=8] {'z'}, dimensions={0} | all-to-all | bytes 1048576 | tf_op jit(solution)/shard_map/all_to_all | solution.py:138
  78.8 0.3 broadcast_in_dim.32
  79.0 0.0 copy-start.1
  79.0 0.0 copy-start.2
  79.1 0.0 copy-start.3
  79.1 32.2 %all_to_all.16 = bf16[4,2048,128]{2,1,0:T(8,128)(2,1)S(1)} all-to-all(bf16[4,2048,128]{2,1,0:T(8,128)(2,1)S(1)} %broadcast_in_dim.32), channel_id=1, replica_groups=mesh['y'=8,'c'=2,'x'=4,'z'=8] {'x'}, dimensions={0} | all-to-all | bytes 4194304 | tf_op jit(solution)/shard_map/all_to_all | solution.py:139
  111.3 0.0 copy-start
  111.3 3.8 %collective-permute-start = (bf16[8192,128]{1,0:T(8,128)(2,1)S(1)}, bf16[8192,128]{1,0:T(8,128)(2,1)}, u32[]{:S(2)}, u32[]{:S(2)}) collective-permute-start(bf16[8192,128]{1,0:T(8,128)(2,1)S(1)} %bitcast.37), channel_id=1, source_target_pairs={{0,32},{32,0},{1,33},{33,1},{2,34},{34,2},{3,35},{35,3},{4,36},{36... | collective-permute-start | bytes 6291464 | tf_op jit(solution)/shard_map/ppermute | solution.py:140
  115.1 0.0 copy-done.1
  115.1 0.0 copy-done.2
  115.1 0.1 fusion
  115.2 0.6 copy.13
  115.9 0.0 copy-done.3
  115.9 0.6 broadcast_in_dim.34.head
  116.4 2.5 %collective-permute-done.other = bf16[8192,128]{1,0:T(8,128)(2,1)} collective-permute-done((bf16[8192,128]{1,0:T(8,128)(2,1)S(1)}, bf16[8192,128]{1,0:T(8,128)(2,1)}, u32[]{:S(2)}, u32[]{:S(2)}) %collective-permute-start) | collective-permute-done | bytes 2097184 | tf_op jit(solution)/shard_map/ppermute | solution.py:140
  119.0 0.0 all-gather.2.cloned.1.call-done.weights_in
  119.0 0.0 copy-done
  119.0 15.9 %score.1 = f32[256]{0:T(256)} custom-call(s32[12288]{0:T(1024)} %bitcast.43, bf16[8192,128]{1,0:T(8,128)(2,1)} %bitcast.38, bf16[8192,128]{1,0:T(8,128)(2,1)} %collective-permute-done.other, bf16[1536,1024]{1,0:T(8,128)(2,1)} %all-gather.2.cloned.1.call-done.weights_in, f32[1,1024]{1,0:T(1,128)} %bitcast.47, bf16[1,1024]{1,0:T(2,128)(2,1)} %broadcast_in_dim.34.head), custom_call_target="tpu_custom_call" | custom-call | tf_op jit(solution)/shard_map/score/pallas_call | solution.py:149
Async XLA Ops:
  7.2 111.8 %all-gather.2.cloned.1.call-start = ((), (), s32[]{:S(2)}) async-start(), calls=%async_computation.3 | async-start | bytes 3244032 | tf_op jit(solution)/shard_map/all_gather | solution.py:116
  9.5 22.5 %all-to-all-start = ((bf16[32,4,128]{2,1,0:T(4,128)(2,1)}), bf16[32,4,128]{2,1,0:T(4,128)(2,1)S(1)}, u32[]{:S(2)}, u32[]{:S(2)}) async-start(bf16[32,4,128]{2,1,0:T(4,128)(2,1)} %bitcast.44), calls=%async_computation | async-start | bytes 65536 | tf_op jit(solution)/shard_map/all_to_all | solution.py:124
  79.0 36.0 %copy-start.1 = (s32[256,24,2]{0,2,1:T(2,128)S(1)}, s32[256,24,2]{0,2,1:T(2,128)}, u32[]{:S(2)}) copy-start(s32[256,24,2]{0,2,1:T(2,128)} %param.15) | copy-start | bytes 147460
  79.0 36.0 %copy-start.2 = (s32[256,24]{0,1:T(8,128)S(1)}, s32[256,24]{0,1:T(8,128)}, u32[]{:S(2)}) copy-start(s32[256,24]{0,1:T(8,128)} %param.16) | copy-start | bytes 73732
  79.1 36.8 %copy-start.3 = (bf16[1024]{0:T(1024)(128)(2,1)S(1)}, bf16[1024]{0:T(1024)(128)(2,1)}, u32[]{:S(2)}) copy-start(bf16[1024]{0:T(1024)(128)(2,1)} %param.19) | copy-start | bytes 6148
  111.3 7.7 %copy-start = (bf16[4,2048,128]{2,1,0:T(8,128)(2,1)}, bf16[4,2048,128]{2,1,0:T(8,128)(2,1)S(1)}, u32[]{:S(2)}) copy-start(bf16[4,2048,128]{2,1,0:T(8,128)(2,1)S(1)} %all_to_all.16) | copy-start | bytes 6291460
  111.3 7.7 %collective-permute-start = (bf16[8192,128]{1,0:T(8,128)(2,1)S(1)}, bf16[8192,128]{1,0:T(8,128)(2,1)}, u32[]{:S(2)}, u32[]{:S(2)}) collective-permute-start(bf16[8192,128]{1,0:T(8,128)(2,1)S(1)} %bitcast.37), channel_id=1, source_target_pairs={{0,32},{32,0},{1,33},{33,1},{2,34},{34,2},{3,35},{35,3},{4,36},{36... | collective-permute-start | bytes 6291464 | tf_op jit(solution)/shard_map/ppermute | solution.py:140
Sparse Core Ops, SparseCore 0:
  11.2 97.4 all-gather.1

commit v3 on v2

v3 whole, which is shorter than its diff:
```python
import jax
import jax.numpy as jnp
from jax import lax
from jax.experimental import pallas as pl
from jax.experimental.pallas import tpu as pltpu
from jax.sharding import Mesh
from jax.sharding import PartitionSpec as P

BF = jnp.bfloat16
F32 = jnp.float32
VMEM = pl.BlockSpec(memory_space=pltpu.VMEM)
HBM = pl.BlockSpec(memory_space=pltpu.HBM)
ANY = pl.BlockSpec(memory_space=pl.ANY)
SMEM = pl.BlockSpec(memory_space=pltpu.SMEM)
HALF = 8192
SMALL = pltpu.CompilerParams(vmem_limit_bytes=36 * 2**20)
LARGE = pltpu.CompilerParams(vmem_limit_bytes=48 * 2**20)


def message_kernel(part, values_t, rows, counts, weights, out, quarters):
    owners, slots = counts.shape[1], rows.shape[1]
    per_owner = slots // owners
    spread = (
        lax.broadcasted_iota(jnp.int32, (owners, slots), 0)
        == lax.broadcasted_iota(jnp.int32, (owners, slots), 1) // per_owner
    ).astype(BF)
    many = jnp.broadcast_to(counts[...].astype(F32), (8, owners)).astype(BF)
    live = jnp.dot(many, spread, preferred_element_type=F32)
    place = lax.broadcasted_iota(jnp.int32, (1, slots), 1) % per_owner
    target = jnp.where(place < live[:1].astype(jnp.int32), rows[...], -64)
    high = jnp.broadcast_to(target >> 5, (64, slots)).astype(F32)
    low = jnp.broadcast_to(target & 31, (64, slots)).astype(F32)
    first = lax.broadcasted_iota(jnp.int32, (64, slots), 0) == 0
    digits = jnp.where(first, high, low)
    out[...] = jnp.concatenate([values_t[...], digits], axis=0).T.astype(BF)
    width = quarters.shape[2]
    mine = weights[:, pl.ds(pl.multiple_of(part[0] * width, width), width)]
    for i in range(quarters.shape[0]):
        quarters[i] = mine


def update_kernel(core, message, state, table_out, accum_out, block):
    rows = state.shape[1]
    total = jnp.zeros((128, rows), F32)
    step = 512
    for start in range(0, message.shape[0], step):
        part = message[start : start + step]
        target = (part[:, 64:65].astype(F32) * 32.0 + part[:, 65:66].astype(F32)).astype(jnp.int32)
        picks = (target == lax.broadcasted_iota(jnp.int32, (step, rows), 1)).astype(F32).astype(BF)
        total += lax.dot_general(part, picks, (((0,), (0,)), ((), ())), preferred_element_type=F32)
    grad = total[:64]
    accum_new = state[64:] + grad * grad
    table_new = state[:64] - 0.5 * grad * lax.rsqrt(accum_new)
    accum_out[...] = accum_new
    table_out[...] = table_new
    stacked = jnp.concatenate([table_new[:, : rows // 2], table_new[:, rows // 2 :]], axis=0)
    mine = jnp.where(core[0] == 0, stacked[:, : rows // 4], stacked[:, rows // 4 :])
    serving = mine.T.astype(BF)
    for i in range(block.shape[0]):
        block[i] = serving


def score_kernel(part, ids_in, own, other, weights_in, bias, head, out, rows, pooled, weights, weight_sems, id_sems, *ids):
    requests = pooled.shape[1]
    id_copies = [
        pltpu.make_async_copy(ids_in.at[pl.ds(i * requests, requests)], to, id_sems.at[i])
        for i, to in enumerate(ids)
    ]
    depth, width = weights.shape[0], weights.shape[1] // 4
    weight_copies = [
        pltpu.make_async_copy(
            weights_in.at[pl.ds(i * depth, depth)],
            weights.at[:, pl.ds(i * width, width)],
            weight_sems.at[i],
        )
        for i in range(4)
    ]
    for copy in id_copies + weight_copies:
        copy.start()
    step = 2048
    for half, at in ((own, 0), (other, HALF)):
        for start in range(0, HALF, step):
            value = half[start : start + step].astype(F32)
            rows[at + start : at + start + step] = value
            rows[2 * HALF + at + start : 2 * HALF + at + start + step] = pltpu.roll(value, 64, 1)
    rows[4 * HALF : 4 * HALF + 8] = jnp.zeros((8, 128), F32)
    left = lax.broadcasted_iota(jnp.int32, (1, 128), 1) < 64
    pairs = pooled.shape[0]
    for copy in id_copies:
        copy.wait()

    def bag(vocab, r):
        return rows[pl.ds(ids[2 * vocab][r], 1), :] + rows[pl.ds(ids[2 * vocab + 1][r], 1), :]

    def look_up(r, carry):
        for j in range(pairs):
            pooled[j, pl.ds(r, 1), :] = jnp.where(left, bag(2 * j, r), bag(2 * j + 1, r))
        return carry

    lax.fori_loop(0, requests, look_up, 0, unroll=4)
    features = jnp.concatenate([pooled[j].astype(BF) for j in range(pairs)], axis=1)
    columns = [pl.ds(pl.multiple_of((part[0] ^ i) * width, width), width) for i in range(4)]
    offset = jnp.concatenate([bias[:, at] for at in columns], axis=1)
    heads = jnp.concatenate([head[:, at].astype(F32) for at in columns], axis=1)
    heads = jnp.broadcast_to(heads, (8, heads.shape[1])).astype(BF)
    for copy in weight_copies:
        copy.wait()
    unit = jnp.dot(features, weights[...], preferred_element_type=F32) + offset
    hidden = (unit / (1.0 + jnp.exp(-unit))).astype(BF)
    scores = lax.dot_general(heads, hidden, (((1,), (1,)), ((), ())), preferred_element_type=F32)
    out[...] = scores[0]


def shift(value, axis, by):
    size = lax.axis_size(axis)
    return lax.ppermute(value, axis, [(i, (i + by) % size) for i in range(size)])


def per_device(
    table,
    accum,
    grad_values,
    grad_rows,
    grad_counts,
    bucket_ids,
    bag_lengths,
    w_hidden,
    b_hidden,
    w_score,
):
    core = lax.axis_index("c")
    part = core * 2 + lax.axis_index("y") % 2
    state = jnp.concatenate([table.T, accum.T], axis=0)
    message, quarters = pl.pallas_call(
        message_kernel,
        out_shape=(jax.ShapeDtypeStruct((128, 128), BF), jax.ShapeDtypeStruct((32, 48, 256), BF)),
        in_specs=[SMEM] + [VMEM] * 4,
        out_specs=(VMEM,) * 2,
        name="message",
    )(part[None], grad_values.T, grad_rows[None, :], grad_counts[None, :], w_hidden)
    got = lax.all_to_all(message.reshape(32, 4, 128), ("x", "z"), 0, 0, tiled=True)
    got, quarters, state = lax.optimization_barrier((got, quarters, state))
    first = lax.all_to_all(quarters, ("x", "z"), 0, 0, tiled=True).reshape(1536, 256)
    slots = lax.all_gather(got, ("y", "c"), axis=0, tiled=True).reshape(2048, 128)
    table_out, accum_out, block = pl.pallas_call(
        update_kernel,
        out_shape=(
            jax.ShapeDtypeStruct((64, 1024), F32),
            jax.ShapeDtypeStruct((64, 1024), F32),
            jax.ShapeDtypeStruct((8, 256, 128), BF),
        ),
        in_specs=[SMEM, VMEM, VMEM],
        out_specs=(VMEM,) * 3,
        compiler_params=SMALL,
        name="update",
    )(core[None], slots, state)
    block, first = lax.optimization_barrier((block, first))
    column = lax.all_to_all(block, "z", 0, 0, tiled=True).reshape(2048, 128)
    upper, lower = shift(first[:768], "y", 1), shift(first[768:], "y", 7)
    column, first, upper, lower = lax.optimization_barrier((column, first, upper, lower))
    swapped = [shift(piece, "c", 1) for piece in (first, upper, lower)]
    columns = jnp.broadcast_to(column[None], (4, 2048, 128))
    own = lax.all_to_all(columns, "x", 0, 0, tiled=True).reshape(HALF, 128)
    weights = jnp.concatenate([first, upper, lower, *swapped], axis=0)
    own, weights = lax.optimization_barrier((own, weights))
    other = shift(own, "c", 1)

    ids = bucket_ids.transpose(1, 2, 0)
    vocab = lax.broadcasted_iota(jnp.int32, ids.shape, 0)
    turned = ((ids >> 9) ^ vocab) & 1
    away = ((ids >> 8) & 1) ^ core
    places = turned * (2 * HALF) + away * HALF + (ids >> 10) * 256 + (ids & 255)
    used = lax.broadcasted_iota(jnp.int32, ids.shape, 1) < bag_lengths.T[:, None, :]
    places = jnp.where(used, places, 4 * HALF)
    scores = pl.pallas_call(
        score_kernel,
        out_shape=jax.ShapeDtypeStruct((256,), F32),
        in_specs=[SMEM] + [HBM] + [VMEM] * 2 + [ANY] + [VMEM] * 2,
        out_specs=VMEM,
        scratch_shapes=[
            pltpu.VMEM((4 * HALF + 8, 128), F32),
            pltpu.VMEM((12, 256, 128), F32),
            pltpu.VMEM((1536, 1024), BF),
            pltpu.SemaphoreType.DMA((4,)),
            pltpu.SemaphoreType.DMA((48,)),
        ]
        + [pltpu.SMEM((256,), jnp.int32)] * 48,
        compiler_params=LARGE,
        name="score",
    )(
        part[None],
        places.reshape(-1),
        own,
        other,
        weights,
        b_hidden[None, :],
        w_score[None, :],
    )
    return (table_out.T, accum_out.T, scores)


def solution(mesh):
    shards = ("x", "z")
    every = ("y", "c", "x", "z")
    inner = Mesh(mesh.devices.reshape(8, 2, 4, 8), every)
    return jax.shard_map(
        per_device,
        mesh=inner,
        in_specs=(
            P(shards, None),
            P(shards, None),
            P(every, None),
            P(every),
            P(every),
            P(every, None, None),
            P(every, None),
            P(shards, None),
            P(),
            P(),
        ),
        out_specs=(P(shards, None), P(shards, None), P(every)),
        check_vma=False,
    )
```

time: 142 us -> 128 us (0.901)
  blocking collectives: 75.5 us -> 21 us
  starting transfers between devices: 17.5 us -> 45.4 us
  waiting for transfers between devices: 12 us -> 35.2 us
  between operations: 14.1 us -> 0.79 us
  local copies, waits for them, and re-layouts: 1.53 us -> 7.7 us
  Pallas kernels: 21.1 us -> 15.9 us
    all_to_all x2 -> x0, blocking collectives: 53.1 us -> none  [the longest x1 32.2 us: per_device(): lax.all_to_all(jnp.broadcast_to(column, (4, 2048, 128)), 'x', 0, 0, tiled...]
    all_to_all x0 -> x3, waiting for transfers between devices: none -> 16.2 us  [the longest x1 12.5 us: per_device(): own = lax.all_to_all(columns, 'x', 0, 0, tiled=True).reshape(HALF, 128)]
    all_to_all x0 -> x3, starting transfers between devices: none -> 14.6 us  [the longest x1 6.6 us: per_device(): column = lax.all_to_all(block, 'z', 0, 0, tiled=True).reshape(2048, 128)]
    ppermute x1 -> x6, starting transfers between devices: 3.76 us -> 17.2 us  [shift(): lax.ppermute(value, axis, [(i, (i + by) % size) for i in range(size)])]
    ppermute x1 -> x6, waiting for transfers between devices: 2.52 us -> 11.3 us  [shift(): lax.ppermute(value, axis, [(i, (i + by) % size) for i in range(size)])]
    unnamed x9 -> x16, local copies, waits for them, and re-layouts: 0.66 us -> 5.24 us
    pallas_call x1, Pallas kernels: 15.9 us -> 11.6 us  [per_device(): pl.pallas_call(score_kernel, out_shape=jax.ShapeDtypeStruct((256,), F32),...]
  transfers between devices with their start and end apart: 3 -> 10, of which waited for: 2 -> 6; matrix products, arithmetic and copies ran while one was open for 1% -> 6% of each run, Pallas kernels for 4% -> 2%
where the time goes in v3:
time: 128 us; the launch traced here: 127 us
  starting transfers between devices  45.4 us (35%)
  waiting for transfers between devices  35.2 us (28%)
  blocking collectives  21 us (16%)
  Pallas kernels  15.9 us (12%)
  local copies, waits for them, and re-layouts  7.7 us (6%)
    all_gather x1, blocking collectives, per_device(): lax.all_gather(got, ('y', 'c'), axis=0, tiled=True).reshape(2048, 128)  21 us
    ppermute x6, starting transfers between devices, shift(): lax.ppermute(value, axis, [(i, (i + by) % size) for i in range(size)])  17.2 us
    all_to_all x1, starting transfers between devices, per_device(): lax.all_to_all(message.reshape(32, 4, 128), ('x', 'z'), 0, 0, tiled=True)  13.7 us
    all_to_all x1, waiting for transfers between devices, per_device(): own = lax.all_to_all(columns, 'x', 0, 0, tiled=True).reshape(HALF, 128)  12.5 us
    pallas_call x1, Pallas kernels, per_device(): pl.pallas_call(score_kernel, out_shape=jax.ShapeDtypeStruct((256,), F32),...  11.6 us
    ppermute x6, waiting for transfers between devices, shift(): lax.ppermute(value, axis, [(i, (i + by) % size) for i in range(size)])  11.3 us
    all_to_all x1, waiting for transfers between devices, per_device(): lax.all_to_all(message.reshape(32, 4, 128), ('x', 'z'), 0, 0, tiled=True)  7.69 us
    all_to_all x1, starting transfers between devices, per_device(): column = lax.all_to_all(block, 'z', 0, 0, tiled=True).reshape(2048, 128)  6.6 us
  transfers between devices with their start and end apart: 10, of which 6 were waited for; matrix products, arithmetic and copies ran while one was open for 6% of the time, Pallas kernels for 2%

profile of v3, /device:TPU:1, one launch (start us, length us, event | category | flops | bytes accessed | tf_op | source)
XLA Modules:
  0.0 127.1 jit_solution(10621407374678754422)
XLA Ops:
  0.6 1.9 %message.1 = (bf16[128,128]{1,0:T(8,128)(2,1)}, bf16[32,48,256]{2,1,0:T(8,128)(2,1)}) custom-call(s32[1]{0:T(128)} %bitcast.1.part, f32[64,128]{1,0:T(8,128)} %bitcast.51, s32[1,128]{1,0:T(1,128)} %bitcast.53, s32[1,32]{1,0:T(1,128)} %bitcast.54, bf16[48,1024]{1,0:T(8,128)(2,1)} %weights.1), custom_call_target="tpu_custom_call" | custom-call | tf_op jit(solution)/shard_map/message/pallas_call | solution.py:134
  2.5 13.7 %all-to-all-start = ((bf16[32,4,128]{2,1,0:T(4,128)(2,1)}), bf16[32,4,128]{2,1,0:T(4,128)(2,1)S(1)}, u32[]{:S(2)}, u32[]{:S(2)}) async-start(bf16[32,4,128]{2,1,0:T(4,128)(2,1)} %bitcast.50), calls=%async_computation | async-start | bytes 65536 | tf_op jit(solution)/shard_map/all_to_all | solution.py:141
  16.3 1.1 pad_maximum_fusion.state
  17.3 7.7 %all-to-all-done = bf16[32,4,128]{2,1,0:T(4,128)(2,1)S(1)} async-done(((bf16[32,4,128]{2,1,0:T(4,128)(2,1)}), bf16[32,4,128]{2,1,0:T(4,128)(2,1)S(1)}, u32[]{:S(2)}, u32[]{:S(2)}) %all-to-all-start) | async-done | bytes 32800 | tf_op jit(solution)/shard_map/all_to_all | solution.py:141
  25.0 3.9 %all-to-all-start.1 = ((bf16[32,48,256]{2,1,0:T(8,128)(2,1)}), bf16[32,48,256]{2,1,0:T(8,128)(2,1)S(1)}, u32[]{:S(2)}, u32[]{:S(2)}) async-start(bf16[32,48,256]{2,1,0:T(8,128)(2,1)} %get-tuple-element.26), calls=%async_computation.1 | async-start | bytes 1572864 | tf_op jit(solution)/shard_map/all_to_all | solution.py:143
  28.9 21.0 %all_gather.3 = bf16[512,4,128]{2,1,0:T(4,128)(2,1)S(1)} all-gather(bf16[32,4,128]{2,1,0:T(4,128)(2,1)S(1)} %all-to-all-done), channel_id=1, replica_groups=mesh['y'=8,'c'=2,'x'=4,'z'=8] {'y','c'}, dimensions={0}, use_global_device_ids=true | all-gather | bytes 557056 | tf_op jit(solution)/shard_map/all_gather | solution.py:144
  49.9 2.4 %update.1 = (f32[64,1024]{1,0:T(8,128)}, f32[64,1024]{1,0:T(8,128)}, bf16[8,256,128]{2,1,0:T(8,128)(2,1)}) custom-call(s32[1]{0:T(128)} %bitcast.core, bf16[2048,128]{1,0:T(8,128)(2,1)S(1)} %bitcast.41, f32[128,1024]{1,0:T(8,128)S(1)} %pad_maximum_fusion.state), custom_call_target="tpu_custom_call" | custom-call | tf_op jit(solution)/shard_map/update/pallas_call | solution.py:145
  52.3 0.0 all-to-all-done.1
  52.3 6.6 %all-to-all-start.2 = ((bf16[8,256,128]{2,1,0:T(8,128)(2,1)}), bf16[8,256,128]{2,1,0:T(8,128)(2,1)S(1)}, u32[]{:S(2)}, u32[]{:S(2)}) async-start(bf16[8,256,128]{2,1,0:T(8,128)(2,1)} %get-tuple-element.27), calls=%async_computation.2 | async-start | bytes 1048576 | tf_op jit(solution)/shard_map/all_to_all | solution.py:158
  58.9 0.1 fusion.3
  58.9 1.9 %collective-permute-start = (bf16[768,256]{1,0:T(8,128)(2,1)S(1)}, bf16[768,256]{1,0:T(8,128)(2,1)S(1)}, u32[]{:S(2)}, u32[]{:S(2)}) collective-permute-start(bf16[768,256]{1,0:T(8,128)(2,1)S(1)} %get-tuple-element.36), channel_id=1, source_target_pairs={{0,64},{64,128},{128,192},{192,256},{256,320},{320,384},{384,448},... | collective-permute-start | bytes 1179656 | tf_op jit(solution)/shard_map/ppermute | solution.py:116
  60.9 4.6 %collective-permute-start.1 = (bf16[768,256]{1,0:T(8,128)(2,1)S(1)}, bf16[768,256]{1,0:T(8,128)(2,1)S(1)}, u32[]{:S(2)}, u32[]{:S(2)}) collective-permute-start(bf16[768,256]{1,0:T(8,128)(2,1)S(1)} %get-tuple-element.35), channel_id=1, source_target_pairs={{0,448},{64,0},{128,64},{192,128},{256,192},{320,256},{384,320},{4... | collective-permute-start | bytes 1179656 | tf_op jit(solution)/shard_map/ppermute | solution.py:116
  65.4 6.8 %collective-permute-done = bf16[768,256]{1,0:T(8,128)(2,1)S(1)} collective-permute-done((bf16[768,256]{1,0:T(8,128)(2,1)S(1)}, bf16[768,256]{1,0:T(8,128)(2,1)S(1)}, u32[]{:S(2)}, u32[]{:S(2)}) %collective-permute-start) | collective-permute-done | bytes 393248 | tf_op jit(solution)/shard_map/ppermute | solution.py:116
  72.3 0.0 copy-start.1
  72.3 0.9 collective-permute-done.1
  73.2 3.7 %all-to-all-done.2 = bf16[8,256,128]{2,1,0:T(8,128)(2,1)S(1)} async-done(((bf16[8,256,128]{2,1,0:T(8,128)(2,1)}), bf16[8,256,128]{2,1,0:T(8,128)(2,1)S(1)}, u32[]{:S(2)}, u32[]{:S(2)}) %all-to-all-start.2) | async-done | bytes 524320 | tf_op jit(solution)/shard_map/all_to_all | solution.py:158
  76.8 1.6 %broadcast_in_dim.35 = bf16[4,2048,128]{2,1,0:T(8,128)(2,1)} broadcast(bf16[2048,128]{1,0:T(8,128)(2,1)S(1)} %bitcast.47), dimensions={1,2} | broadcast | bytes 2621440 | tf_op jit(solution)/shard_map/broadcast_in_dim | solution.py:162
  78.5 0.0 copy-done.1
  78.5 4.1 %all-to-all-start.3 = ((bf16[4,2048,128]{2,1,0:T(8,128)(2,1)}), bf16[4,2048,128]{2,1,0:T(8,128)(2,1)S(1)}, u32[]{:S(2)}, u32[]{:S(2)}) async-start(bf16[4,2048,128]{2,1,0:T(8,128)(2,1)} %broadcast_in_dim.35), calls=%async_computation.3 | async-start | bytes 4194304 | tf_op jit(solution)/shard_map/all_to_all | solution.py:163
  82.5 0.0 copy-start.2
  82.6 0.0 copy-start.3
  82.6 0.0 copy-start.4
  82.6 0.0 copy-start
  82.6 2.8 %collective-permute-start.2 = (bf16[1536,256]{1,0:T(8,128)(2,1)S(1)}, bf16[1536,256]{1,0:T(8,128)(2,1)S(1)}, u32[]{:S(2)}, u32[]{:S(2)}) collective-permute-start(bf16[1536,256]{1,0:T(8,128)(2,1)S(1)} %bitcast.45), channel_id=1, source_target_pairs={{0,32},{32,0},{1,33},{33,1},{2,34},{34,2},{3,35},{35,3},{4,36},{36... | collective-permute-start | bytes 2359304 | tf_op jit(solution)/shard_map/ppermute | solution.py:116
  85.4 1.9 %collective-permute-start.3 = (bf16[768,256]{1,0:T(8,128)(2,1)}, bf16[768,256]{1,0:T(8,128)(2,1)S(1)}, u32[]{:S(2)}, u32[]{:S(2)}) collective-permute-start(bf16[768,256]{1,0:T(8,128)(2,1)} %copy-done.1), channel_id=1, source_target_pairs={{0,32},{32,0},{1,33},{33,1},{2,34},{34,2},{3,35},{35,3},{4,36},{36... | collective-permute-start | bytes 1179656 | tf_op jit(solution)/shard_map/ppermute | solution.py:116
  87.3 0.9 constant_dynamic-update-slice_fusion.5
  88.2 1.8 %constant_dynamic-update-slice_fusion.4 = bf16[6144,256]{1,0:T(8,128)(2,1)} fusion(bf16[6144,256]{1,0:T(8,128)(2,1)} %constant_dynamic-update-slice_fusion.5, bf16[768,256]{1,0:T(8,128)(2,1)} %copy-done.1), kind=kLoop, calls=%fused_computation.13 | loop fusion | bytes 786432
  90.0 2.4 %collective-permute-start.4 = (bf16[768,256]{1,0:T(8,128)(2,1)S(1)}, bf16[768,256]{1,0:T(8,128)(2,1)S(1)}, u32[]{:S(2)}, u32[]{:S(2)}) collective-permute-start(bf16[768,256]{1,0:T(8,128)(2,1)S(1)} %collective-permute-done.1), channel_id=1, source_target_pairs={{0,32},{32,0},{1,33},{33,1},{2,34},{34,2},{3,35},{35,3},{4,36},{36... | collective-permute-start | bytes 1179656 | tf_op jit(solution)/shard_map/ppermute | solution.py:116
  92.4 0.8 constant_dynamic-update-slice_fusion.3
  93.2 0.0 collective-permute-done.2
  93.2 0.9 constant_dynamic-update-slice_fusion.2
  94.1 0.0 collective-permute-done.3
  94.1 0.8 constant_dynamic-update-slice_fusion.1
  94.9 0.0 collective-permute-done.4
  94.9 0.8 constant_dynamic-update-slice_fusion.weights_in
  95.7 12.5 %all-to-all-done.3 = bf16[4,2048,128]{2,1,0:T(8,128)(2,1)S(1)} async-done(((bf16[4,2048,128]{2,1,0:T(8,128)(2,1)}), bf16[4,2048,128]{2,1,0:T(8,128)(2,1)S(1)}, u32[]{:S(2)}, u32[]{:S(2)}) %all-to-all-start.3) | async-done | bytes 2097184 | tf_op jit(solution)/shard_map/all_to_all | solution.py:163
  108.2 3.5 %collective-permute-start.5 = (bf16[8192,128]{1,0:T(8,128)(2,1)S(1)}, bf16[8192,128]{1,0:T(8,128)(2,1)S(1)}, u32[]{:S(2)}, u32[]{:S(2)}) collective-permute-start(bf16[8192,128]{1,0:T(8,128)(2,1)S(1)} %bitcast.39), channel_id=1, source_target_pairs={{0,32},{32,0},{1,33},{33,1},{2,34},{34,2},{3,35},{35,3},{4,36},{36... | collective-permute-start | bytes 6291464 | tf_op jit(solution)/shard_map/ppermute | solution.py:116
  111.7 0.0 copy-done.2
  111.8 0.0 copy-done.3
  111.8 0.1 fusion
  111.9 0.0 copy-done.4
  111.9 3.6 %collective-permute-done.5.other = bf16[8192,128]{1,0:T(8,128)(2,1)S(1)} collective-permute-done((bf16[8192,128]{1,0:T(8,128)(2,1)S(1)}, bf16[8192,128]{1,0:T(8,128)(2,1)S(1)}, u32[]{:S(2)}, u32[]{:S(2)}) %collective-permute-start.5) | collective-permute-done | bytes 2097184 | tf_op jit(solution)/shard_map/ppermute | solution.py:116
  115.5 0.0 copy-done
  115.5 11.6 %score.1 = f32[256]{0:T(256)} custom-call(s32[1]{0:T(128)} %bitcast.1.part, s32[12288]{0:T(1024)S(1)} %bitcast.42, bf16[8192,128]{1,0:T(8,128)(2,1)S(1)} %bitcast.40, bf16[8192,128]{1,0:T(8,128)(2,1)S(1)} %collective-permute-done.5.other, bf16[6144,256]{1,0:T(8,128)(2,1)} %constant_dynamic-update-slice_fusion.weights_in, f32[1,1024]{1,0:T(1,128)S(1)} %bitcast.43, ...), custom_call_target="tpu_custom_call" | custom-call | tf_op jit(solution)/shard_map/score/pallas_call | solution.py:175
  (2 shorter events, 0.0 us)
Async XLA Ops:
  2.5 22.5 %all-to-all-start = ((bf16[32,4,128]{2,1,0:T(4,128)(2,1)}), bf16[32,4,128]{2,1,0:T(4,128)(2,1)S(1)}, u32[]{:S(2)}, u32[]{:S(2)}) async-start(bf16[32,4,128]{2,1,0:T(4,128)(2,1)} %bitcast.50), calls=%async_computation | async-start | bytes 65536 | tf_op jit(solution)/shard_map/all_to_all | solution.py:141
  25.0 27.3 %all-to-all-start.1 = ((bf16[32,48,256]{2,1,0:T(8,128)(2,1)}), bf16[32,48,256]{2,1,0:T(8,128)(2,1)S(1)}, u32[]{:S(2)}, u32[]{:S(2)}) async-start(bf16[32,48,256]{2,1,0:T(8,128)(2,1)} %get-tuple-element.26), calls=%async_computation.1 | async-start | bytes 1572864 | tf_op jit(solution)/shard_map/all_to_all | solution.py:143
  52.3 24.6 %all-to-all-start.2 = ((bf16[8,256,128]{2,1,0:T(8,128)(2,1)}), bf16[8,256,128]{2,1,0:T(8,128)(2,1)S(1)}, u32[]{:S(2)}, u32[]{:S(2)}) async-start(bf16[8,256,128]{2,1,0:T(8,128)(2,1)} %get-tuple-element.27), calls=%async_computation.2 | async-start | bytes 1048576 | tf_op jit(solution)/shard_map/all_to_all | solution.py:158
  58.9 13.4 %collective-permute-start = (bf16[768,256]{1,0:T(8,128)(2,1)S(1)}, bf16[768,256]{1,0:T(8,128)(2,1)S(1)}, u32[]{:S(2)}, u32[]{:S(2)}) collective-permute-start(bf16[768,256]{1,0:T(8,128)(2,1)S(1)} %get-tuple-element.36), channel_id=1, source_target_pairs={{0,64},{64,128},{128,192},{192,256},{256,320},{320,384},{384,448},... | collective-permute-start | bytes 1179656 | tf_op jit(solution)/shard_map/ppermute | solution.py:116
  60.9 12.3 %collective-permute-start.1 = (bf16[768,256]{1,0:T(8,128)(2,1)S(1)}, bf16[768,256]{1,0:T(8,128)(2,1)S(1)}, u32[]{:S(2)}, u32[]{:S(2)}) collective-permute-start(bf16[768,256]{1,0:T(8,128)(2,1)S(1)} %get-tuple-element.35), channel_id=1, source_target_pairs={{0,448},{64,0},{128,64},{192,128},{256,192},{320,256},{384,320},{4... | collective-permute-start | bytes 1179656 | tf_op jit(solution)/shard_map/ppermute | solution.py:116
  72.3 6.2 %copy-start.1 = (bf16[768,256]{1,0:T(8,128)(2,1)}, bf16[768,256]{1,0:T(8,128)(2,1)S(1)}, u32[]{:S(2)}) copy-start(bf16[768,256]{1,0:T(8,128)(2,1)S(1)} %collective-permute-done) | copy-start | bytes 1179652
  78.5 29.7 %all-to-all-start.3 = ((bf16[4,2048,128]{2,1,0:T(8,128)(2,1)}), bf16[4,2048,128]{2,1,0:T(8,128)(2,1)S(1)}, u32[]{:S(2)}, u32[]{:S(2)}) async-start(bf16[4,2048,128]{2,1,0:T(8,128)(2,1)} %broadcast_in_dim.35), calls=%async_computation.3 | async-start | bytes 4194304 | tf_op jit(solution)/shard_map/all_to_all | solution.py:163
  82.5 29.2 %copy-start.2 = (s32[256,24,2]{0,2,1:T(2,128)S(1)}, s32[256,24,2]{0,2,1:T(2,128)}, u32[]{:S(2)}) copy-start(s32[256,24,2]{0,2,1:T(2,128)} %param.15) | copy-start | bytes 147460
  82.6 29.2 %copy-start.3 = (s32[256,24]{0,1:T(8,128)S(1)}, s32[256,24]{0,1:T(8,128)}, u32[]{:S(2)}) copy-start(s32[256,24]{0,1:T(8,128)} %param.16) | copy-start | bytes 73732
  82.6 29.4 %copy-start.4 = (bf16[1024]{0:T(1024)(128)(2,1)S(1)}, bf16[1024]{0:T(1024)(128)(2,1)}, u32[]{:S(2)}) copy-start(bf16[1024]{0:T(1024)(128)(2,1)} %param.19) | copy-start | bytes 6148
  82.6 32.9 %copy-start = (f32[1024]{0:T(1024)S(1)}, f32[1024]{0:T(1024)}, u32[]{:S(2)}) copy-start(f32[1024]{0:T(1024)} %param.18) | copy-start | bytes 12292
  82.6 10.6 %collective-permute-start.2 = (bf16[1536,256]{1,0:T(8,128)(2,1)S(1)}, bf16[1536,256]{1,0:T(8,128)(2,1)S(1)}, u32[]{:S(2)}, u32[]{:S(2)}) collective-permute-start(bf16[1536,256]{1,0:T(8,128)(2,1)S(1)} %bitcast.45), channel_id=1, source_target_pairs={{0,32},{32,0},{1,33},{33,1},{2,34},{34,2},{3,35},{35,3},{4,36},{36... | collective-permute-start | bytes 2359304 | tf_op jit(solution)/shard_map/ppermute | solution.py:116
  85.4 8.7 %collective-permute-start.3 = (bf16[768,256]{1,0:T(8,128)(2,1)}, bf16[768,256]{1,0:T(8,128)(2,1)S(1)}, u32[]{:S(2)}, u32[]{:S(2)}) collective-permute-start(bf16[768,256]{1,0:T(8,128)(2,1)} %copy-done.1), channel_id=1, source_target_pairs={{0,32},{32,0},{1,33},{33,1},{2,34},{34,2},{3,35},{35,3},{4,36},{36... | collective-permute-start | bytes 1179656 | tf_op jit(solution)/shard_map/ppermute | solution.py:116
  90.0 4.9 %collective-permute-start.4 = (bf16[768,256]{1,0:T(8,128)(2,1)S(1)}, bf16[768,256]{1,0:T(8,128)(2,1)S(1)}, u32[]{:S(2)}, u32[]{:S(2)}) collective-permute-start(bf16[768,256]{1,0:T(8,128)(2,1)S(1)} %collective-permute-done.1), channel_id=1, source_target_pairs={{0,32},{32,0},{1,33},{33,1},{2,34},{34,2},{3,35},{35,3},{4,36},{36... | collective-permute-start | bytes 1179656 | tf_op jit(solution)/shard_map/ppermute | solution.py:116
  108.2 7.3 %collective-permute-start.5 = (bf16[8192,128]{1,0:T(8,128)(2,1)S(1)}, bf16[8192,128]{1,0:T(8,128)(2,1)S(1)}, u32[]{:S(2)}, u32[]{:S(2)}) collective-permute-start(bf16[8192,128]{1,0:T(8,128)(2,1)S(1)} %bitcast.39), channel_id=1, source_target_pairs={{0,32},{32,0},{1,33},{33,1},{2,34},{34,2},{3,35},{35,3},{4,36},{36... | collective-permute-start | bytes 6291464 | tf_op jit(solution)/shard_map/ppermute | solution.py:116

commit v4 on v3

--- a/solution.py
+++ b/solution.py
@@ -156,8 +156,8 @@
     )(core[None], slots, state)
     block, first = lax.optimization_barrier((block, first))
     column = lax.all_to_all(block, "z", 0, 0, tiled=True).reshape(2048, 128)
+    column, first = lax.optimization_barrier((column, first))
     upper, lower = shift(first[:768], "y", 1), shift(first[768:], "y", 7)
-    column, first, upper, lower = lax.optimization_barrier((column, first, upper, lower))
     swapped = [shift(piece, "c", 1) for piece in (first, upper, lower)]
     columns = jnp.broadcast_to(column[None], (4, 2048, 128))
     own = lax.all_to_all(columns, "x", 0, 0, tiled=True).reshape(HALF, 128)

time: 128 us -> 127 us (level)
  blocking collectives: 21 us -> 45.2 us
  waiting for transfers between devices: 35.2 us -> 17.7 us
  starting transfers between devices: 45.4 us -> 39.3 us
    all_to_all x0 -> x1, blocking collectives: none -> 24.3 us  [per_device(): column = lax.all_to_all(block, 'z', 0, 0, tiled=True).reshape(2048, 128)]
    all_to_all x1, waiting for transfers between devices: 12.5 us -> 0.2 us  [per_device(): own = lax.all_to_all(columns, 'x', 0, 0, tiled=True).reshape(HALF, 128)]
    all_to_all x1 -> x0, starting transfers between devices: 6.6 us -> none  [per_device(): column = lax.all_to_all(block, 'z', 0, 0, tiled=True).reshape(2048, 128)]
    all_to_all x1 -> x0, waiting for transfers between devices: 3.7 us -> none  [per_device(): column = lax.all_to_all(block, 'z', 0, 0, tiled=True).reshape(2048, 128)]
    ppermute x6, waiting for transfers between devices: 11.3 us -> 9.79 us  [shift(): lax.ppermute(value, axis, [(i, (i + by) % size) for i in range(size)])]
    unnamed x16 -> x14, local copies, waits for them, and re-layouts: 5.24 us -> 4.27 us
  transfers between devices with their start and end apart: 10 -> 9, of which waited for: 6 -> 4; matrix products, arithmetic and copies ran while one was open for 6% -> 5% of each run, Pallas kernels for 2% -> 2%
where the time goes in v4:
time: 127 us
  blocking collectives  45.2 us (36%)
  starting transfers between devices  39.3 us (31%)
  waiting for transfers between devices  17.7 us (14%)
  Pallas kernels  15.7 us (12%)
  local copies, waits for them, and re-layouts  6.75 us (5%)
    all_to_all x1, blocking collectives, per_device(): column = lax.all_to_all(block, 'z', 0, 0, tiled=True).reshape(2048, 128)  24.3 us
    all_gather x1, blocking collectives, per_device(): lax.all_gather(got, ('y', 'c'), axis=0, tiled=True).reshape(2048, 128)  21 us
    ppermute x6, starting transfers between devices, shift(): lax.ppermute(value, axis, [(i, (i + by) % size) for i in range(size)])  17.6 us
    all_to_all x1, starting transfers between devices, per_device(): lax.all_to_all(message.reshape(32, 4, 128), ('x', 'z'), 0, 0, tiled=True)  13.7 us
    pallas_call x1, Pallas kernels, per_device(): pl.pallas_call(score_kernel, out_shape=jax.ShapeDtypeStruct((256,), F32),...  11.6 us
    ppermute x6, waiting for transfers between devices, shift(): lax.ppermute(value, axis, [(i, (i + by) % size) for i in range(size)])  9.79 us
    all_to_all x1, waiting for transfers between devices, per_device(): lax.all_to_all(message.reshape(32, 4, 128), ('x', 'z'), 0, 0, tiled=True)  7.69 us
    unnamed x14, local copies, waits for them, and re-layouts  4.27 us
  transfers between devices with their start and end apart: 9, of which 4 were waited for; matrix products, arithmetic and copies ran while one was open for 5% of the time, Pallas kernels for 2%

profile of v4, /device:TPU:1, one launch (start us, length us, event | category | flops | bytes accessed | tf_op | source)
XLA Modules:
  0.0 126.7 jit_solution(17576663869946546345)
XLA Ops:
  0.6 1.9 %message.1 = (bf16[128,128]{1,0:T(8,128)(2,1)}, bf16[32,48,256]{2,1,0:T(8,128)(2,1)}) custom-call(s32[1]{0:T(128)} %bitcast.1.part, f32[64,128]{1,0:T(8,128)} %bitcast.51, s32[1,128]{1,0:T(1,128)} %bitcast.53, s32[1,32]{1,0:T(1,128)} %bitcast.54, bf16[48,1024]{1,0:T(8,128)(2,1)} %weights.1), custom_call_target="tpu_custom_call" | custom-call | tf_op jit(solution)/shard_map/message/pallas_call | solution.py:134
  2.5 13.7 %all-to-all-start = ((bf16[32,4,128]{2,1,0:T(4,128)(2,1)}), bf16[32,4,128]{2,1,0:T(4,128)(2,1)S(1)}, u32[]{:S(2)}, u32[]{:S(2)}) async-start(bf16[32,4,128]{2,1,0:T(4,128)(2,1)} %bitcast.50), calls=%async_computation | async-start | bytes 65536 | tf_op jit(solution)/shard_map/all_to_all | solution.py:141
  16.3 1.1 pad_maximum_fusion.state
  17.3 7.7 %all-to-all-done = bf16[32,4,128]{2,1,0:T(4,128)(2,1)S(1)} async-done(((bf16[32,4,128]{2,1,0:T(4,128)(2,1)}), bf16[32,4,128]{2,1,0:T(4,128)(2,1)S(1)}, u32[]{:S(2)}, u32[]{:S(2)}) %all-to-all-start) | async-done | bytes 32800 | tf_op jit(solution)/shard_map/all_to_all | solution.py:141
  25.0 3.9 %all-to-all-start.1 = ((bf16[32,48,256]{2,1,0:T(8,128)(2,1)}), bf16[32,48,256]{2,1,0:T(8,128)(2,1)S(1)}, u32[]{:S(2)}, u32[]{:S(2)}) async-start(bf16[32,48,256]{2,1,0:T(8,128)(2,1)} %get-tuple-element.24), calls=%async_computation.1 | async-start | bytes 1572864 | tf_op jit(solution)/shard_map/all_to_all | solution.py:143
  28.9 21.0 %all_gather.3 = bf16[512,4,128]{2,1,0:T(4,128)(2,1)S(1)} all-gather(bf16[32,4,128]{2,1,0:T(4,128)(2,1)S(1)} %all-to-all-done), channel_id=1, replica_groups=mesh['y'=8,'c'=2,'x'=4,'z'=8] {'y','c'}, dimensions={0}, use_global_device_ids=true | all-gather | bytes 557056 | tf_op jit(solution)/shard_map/all_gather | solution.py:144
  49.9 2.2 %update.1 = (f32[64,1024]{1,0:T(8,128)}, f32[64,1024]{1,0:T(8,128)}, bf16[8,256,128]{2,1,0:T(8,128)(2,1)S(1)}) custom-call(s32[1]{0:T(128)} %bitcast.core, bf16[2048,128]{1,0:T(8,128)(2,1)S(1)} %bitcast.41, f32[128,1024]{1,0:T(8,128)S(1)} %pad_maximum_fusion.state), custom_call_target="tpu_custom_call" | custom-call | tf_op jit(solution)/shard_map/update/pallas_call | solution.py:145
  52.1 0.0 all-to-all-done.1
  52.1 24.3 %all_to_all.20 = bf16[8,256,128]{2,1,0:T(8,128)(2,1)S(1)} all-to-all(bf16[8,256,128]{2,1,0:T(8,128)(2,1)S(1)} %get-tuple-element.25), channel_id=1, replica_groups=mesh['y'=8,'c'=2,'x'=4,'z'=8] {'z'}, dimensions={0} | all-to-all | bytes 1048576 | tf_op jit(solution)/shard_map/all_to_all | solution.py:158
  76.4 1.6 %broadcast_in_dim.35 = bf16[4,2048,128]{2,1,0:T(8,128)(2,1)} broadcast(bf16[2048,128]{1,0:T(8,128)(2,1)S(1)} %bitcast.47), dimensions={1,2} | broadcast | bytes 2621440 | tf_op jit(solution)/shard_map/broadcast_in_dim | solution.py:162
  78.0 4.1 %all-to-all-start.3 = ((bf16[4,2048,128]{2,1,0:T(8,128)(2,1)}), bf16[4,2048,128]{2,1,0:T(8,128)(2,1)S(1)}, u32[]{:S(2)}, u32[]{:S(2)}) async-start(bf16[4,2048,128]{2,1,0:T(8,128)(2,1)} %broadcast_in_dim.35), calls=%async_computation.3 | async-start | bytes 4194304 | tf_op jit(solution)/shard_map/all_to_all | solution.py:163
  82.1 2.7 %collective-permute-start.2 = (bf16[1536,256]{1,0:T(8,128)(2,1)S(1)}, bf16[1536,256]{1,0:T(8,128)(2,1)S(1)}, u32[]{:S(2)}, u32[]{:S(2)}) collective-permute-start(bf16[1536,256]{1,0:T(8,128)(2,1)S(1)} %bitcast.44), channel_id=1, source_target_pairs={{0,32},{32,0},{1,33},{33,1},{2,34},{34,2},{3,35},{35,3},{4,36},{36... | collective-permute-start | bytes 2359304 | tf_op jit(solution)/shard_map/ppermute | solution.py:116
  84.8 0.1 fusion.3
  84.9 1.9 %collective-permute-start = (bf16[768,256]{1,0:T(8,128)(2,1)S(1)}, bf16[768,256]{1,0:T(8,128)(2,1)S(1)}, u32[]{:S(2)}, u32[]{:S(2)}) collective-permute-start(bf16[768,256]{1,0:T(8,128)(2,1)S(1)} %get-tuple-element.32), channel_id=1, source_target_pairs={{0,64},{64,128},{128,192},{192,256},{256,320},{320,384},{384,448},... | collective-permute-start | bytes 1179656 | tf_op jit(solution)/shard_map/ppermute | solution.py:116
  86.8 0.0 copy-start.1
  86.8 0.0 copy-start.2
  86.8 0.0 copy-start.3
  86.9 0.0 copy-start
  86.9 4.7 %collective-permute-start.1 = (bf16[768,256]{1,0:T(8,128)(2,1)S(1)}, bf16[768,256]{1,0:T(8,128)(2,1)S(1)}, u32[]{:S(2)}, u32[]{:S(2)}) collective-permute-start(bf16[768,256]{1,0:T(8,128)(2,1)S(1)} %get-tuple-element.31), channel_id=1, source_target_pairs={{0,448},{64,0},{128,64},{192,128},{256,192},{320,256},{384,320},{4... | collective-permute-start | bytes 1179656 | tf_op jit(solution)/shard_map/ppermute | solution.py:116
  91.6 0.9 constant_dynamic-update-slice_fusion.5
  92.5 6.2 %collective-permute-done = bf16[768,256]{1,0:T(8,128)(2,1)S(1)} collective-permute-done((bf16[768,256]{1,0:T(8,128)(2,1)S(1)}, bf16[768,256]{1,0:T(8,128)(2,1)S(1)}, u32[]{:S(2)}, u32[]{:S(2)}) %collective-permute-start) | collective-permute-done | bytes 393248 | tf_op jit(solution)/shard_map/ppermute | solution.py:116
  98.7 2.7 %collective-permute-start.3 = (bf16[768,256]{1,0:T(8,128)(2,1)S(1)}, bf16[768,256]{1,0:T(8,128)(2,1)S(1)}, u32[]{:S(2)}, u32[]{:S(2)}) collective-permute-start(bf16[768,256]{1,0:T(8,128)(2,1)S(1)} %collective-permute-done), channel_id=1, source_target_pairs={{0,32},{32,0},{1,33},{33,1},{2,34},{34,2},{3,35},{35,3},{4,36},{36... | collective-permute-start | bytes 1179656 | tf_op jit(solution)/shard_map/ppermute | solution.py:116
  101.4 0.8 constant_dynamic-update-slice_fusion.4
  102.2 0.0 collective-permute-done.1
  102.2 1.9 %collective-permute-start.4 = (bf16[768,256]{1,0:T(8,128)(2,1)S(1)}, bf16[768,256]{1,0:T(8,128)(2,1)S(1)}, u32[]{:S(2)}, u32[]{:S(2)}) collective-permute-start(bf16[768,256]{1,0:T(8,128)(2,1)S(1)} %collective-permute-done.1), channel_id=1, source_target_pairs={{0,32},{32,0},{1,33},{33,1},{2,34},{34,2},{3,35},{35,3},{4,36},{36... | collective-permute-start | bytes 1179656 | tf_op jit(solution)/shard_map/ppermute | solution.py:116
  104.1 0.8 constant_dynamic-update-slice_fusion.3
  104.9 0.0 collective-permute-done.2
  104.9 0.9 constant_dynamic-update-slice_fusion.2
  105.9 0.0 collective-permute-done.3
  105.9 0.8 constant_dynamic-update-slice_fusion.1
  106.6 0.0 collective-permute-done.4
  106.6 0.8 constant_dynamic-update-slice_fusion.weights_in
  107.4 0.2 all-to-all-done.3
  107.6 3.6 %collective-permute-start.5 = (bf16[8192,128]{1,0:T(8,128)(2,1)S(1)}, bf16[8192,128]{1,0:T(8,128)(2,1)S(1)}, u32[]{:S(2)}, u32[]{:S(2)}) collective-permute-start(bf16[8192,128]{1,0:T(8,128)(2,1)S(1)} %bitcast.39), channel_id=1, source_target_pairs={{0,32},{32,0},{1,33},{33,1},{2,34},{34,2},{3,35},{35,3},{4,36},{36... | collective-permute-start | bytes 6291464 | tf_op jit(solution)/shard_map/ppermute | solution.py:116
  111.3 0.0 copy-done.1
  111.3 0.0 copy-done.2
  111.3 0.1 fusion
  111.4 0.0 copy-done.3
  111.5 3.6 %collective-permute-done.5.other = bf16[8192,128]{1,0:T(8,128)(2,1)S(1)} collective-permute-done((bf16[8192,128]{1,0:T(8,128)(2,1)S(1)}, bf16[8192,128]{1,0:T(8,128)(2,1)S(1)}, u32[]{:S(2)}, u32[]{:S(2)}) %collective-permute-start.5) | collective-permute-done | bytes 2097184 | tf_op jit(solution)/shard_map/ppermute | solution.py:116
  115.0 0.0 copy-done
  115.0 11.6 %score.1 = f32[256]{0:T(256)} custom-call(s32[1]{0:T(128)} %bitcast.1.part, s32[12288]{0:T(1024)S(1)} %bitcast.42, bf16[8192,128]{1,0:T(8,128)(2,1)S(1)} %bitcast.40, bf16[8192,128]{1,0:T(8,128)(2,1)S(1)} %collective-permute-done.5.other, bf16[6144,256]{1,0:T(8,128)(2,1)} %constant_dynamic-update-slice_fusion.weights_in, f32[1,1024]{1,0:T(1,128)S(1)} %bitcast.43, ...), custom_call_target="tpu_custom_call" | custom-call | tf_op jit(solution)/shard_map/score/pallas_call | solution.py:175
  (2 shorter events, 0.0 us)
Async XLA Ops:
  2.5 22.5 %all-to-all-start = ((bf16[32,4,128]{2,1,0:T(4,128)(2,1)}), bf16[32,4,128]{2,1,0:T(4,128)(2,1)S(1)}, u32[]{:S(2)}, u32[]{:S(2)}) async-start(bf16[32,4,128]{2,1,0:T(4,128)(2,1)} %bitcast.50), calls=%async_computation | async-start | bytes 65536 | tf_op jit(solution)/shard_map/all_to_all | solution.py:141
  25.0 27.1 %all-to-all-start.1 = ((bf16[32,48,256]{2,1,0:T(8,128)(2,1)}), bf16[32,48,256]{2,1,0:T(8,128)(2,1)S(1)}, u32[]{:S(2)}, u32[]{:S(2)}) async-start(bf16[32,48,256]{2,1,0:T(8,128)(2,1)} %get-tuple-element.24), calls=%async_computation.1 | async-start | bytes 1572864 | tf_op jit(solution)/shard_map/all_to_all | solution.py:143
  78.0 29.6 %all-to-all-start.3 = ((bf16[4,2048,128]{2,1,0:T(8,128)(2,1)}), bf16[4,2048,128]{2,1,0:T(8,128)(2,1)S(1)}, u32[]{:S(2)}, u32[]{:S(2)}) async-start(bf16[4,2048,128]{2,1,0:T(8,128)(2,1)} %broadcast_in_dim.35), calls=%async_computation.3 | async-start | bytes 4194304 | tf_op jit(solution)/shard_map/all_to_all | solution.py:163
  82.1 22.8 %collective-permute-start.2 = (bf16[1536,256]{1,0:T(8,128)(2,1)S(1)}, bf16[1536,256]{1,0:T(8,128)(2,1)S(1)}, u32[]{:S(2)}, u32[]{:S(2)}) collective-permute-start(bf16[1536,256]{1,0:T(8,128)(2,1)S(1)} %bitcast.44), channel_id=1, source_target_pairs={{0,32},{32,0},{1,33},{33,1},{2,34},{34,2},{3,35},{35,3},{4,36},{36... | collective-permute-start | bytes 2359304 | tf_op jit(solution)/shard_map/ppermute | solution.py:116
  84.9 13.8 %collective-permute-start = (bf16[768,256]{1,0:T(8,128)(2,1)S(1)}, bf16[768,256]{1,0:T(8,128)(2,1)S(1)}, u32[]{:S(2)}, u32[]{:S(2)}) collective-permute-start(bf16[768,256]{1,0:T(8,128)(2,1)S(1)} %get-tuple-element.32), channel_id=1, source_target_pairs={{0,64},{64,128},{128,192},{192,256},{256,320},{320,384},{384,448},... | collective-permute-start | bytes 1179656 | tf_op jit(solution)/shard_map/ppermute | solution.py:116
  86.8 24.5 %copy-start.1 = (s32[256,24,2]{0,2,1:T(2,128)S(1)}, s32[256,24,2]{0,2,1:T(2,128)}, u32[]{:S(2)}) copy-start(s32[256,24,2]{0,2,1:T(2,128)} %param.15) | copy-start | bytes 147460
  86.8 24.5 %copy-start.2 = (s32[256,24]{0,1:T(8,128)S(1)}, s32[256,24]{0,1:T(8,128)}, u32[]{:S(2)}) copy-start(s32[256,24]{0,1:T(8,128)} %param.16) | copy-start | bytes 73732
  86.8 24.6 %copy-start.3 = (bf16[1024]{0:T(1024)(128)(2,1)S(1)}, bf16[1024]{0:T(1024)(128)(2,1)}, u32[]{:S(2)}) copy-start(bf16[1024]{0:T(1024)(128)(2,1)} %param.19) | copy-start | bytes 6148
  86.9 28.2 %copy-start = (f32[1024]{0:T(1024)S(1)}, f32[1024]{0:T(1024)}, u32[]{:S(2)}) copy-start(f32[1024]{0:T(1024)} %param.18) | copy-start | bytes 12292
  86.9 15.4 %collective-permute-start.1 = (bf16[768,256]{1,0:T(8,128)(2,1)S(1)}, bf16[768,256]{1,0:T(8,128)(2,1)S(1)}, u32[]{:S(2)}, u32[]{:S(2)}) collective-permute-start(bf16[768,256]{1,0:T(8,128)(2,1)S(1)} %get-tuple-element.31), channel_id=1, source_target_pairs={{0,448},{64,0},{128,64},{192,128},{256,192},{320,256},{384,320},{4... | collective-permute-start | bytes 1179656 | tf_op jit(solution)/shard_map/ppermute | solution.py:116
  98.7 7.1 %collective-permute-start.3 = (bf16[768,256]{1,0:T(8,128)(2,1)S(1)}, bf16[768,256]{1,0:T(8,128)(2,1)S(1)}, u32[]{:S(2)}, u32[]{:S(2)}) collective-permute-start(bf16[768,256]{1,0:T(8,128)(2,1)S(1)} %collective-permute-done), channel_id=1, source_target_pairs={{0,32},{32,0},{1,33},{33,1},{2,34},{34,2},{3,35},{35,3},{4,36},{36... | collective-permute-start | bytes 1179656 | tf_op jit(solution)/shard_map/ppermute | solution.py:116
  102.2 4.4 %collective-permute-start.4 = (bf16[768,256]{1,0:T(8,128)(2,1)S(1)}, bf16[768,256]{1,0:T(8,128)(2,1)S(1)}, u32[]{:S(2)}, u32[]{:S(2)}) collective-permute-start(bf16[768,256]{1,0:T(8,128)(2,1)S(1)} %collective-permute-done.1), channel_id=1, source_target_pairs={{0,32},{32,0},{1,33},{33,1},{2,34},{34,2},{3,35},{35,3},{4,36},{36... | collective-permute-start | bytes 1179656 | tf_op jit(solution)/shard_map/ppermute | solution.py:116
  107.6 7.4 %collective-permute-start.5 = (bf16[8192,128]{1,0:T(8,128)(2,1)S(1)}, bf16[8192,128]{1,0:T(8,128)(2,1)S(1)}, u32[]{:S(2)}, u32[]{:S(2)}) collective-permute-start(bf16[8192,128]{1,0:T(8,128)(2,1)S(1)} %bitcast.39), channel_id=1, source_target_pairs={{0,32},{32,0},{1,33},{33,1},{2,34},{34,2},{3,35},{35,3},{4,36},{36... | collective-permute-start | bytes 6291464 | tf_op jit(solution)/shard_map/ppermute | solution.py:116

commit v5 on v4

--- a/solution.py
+++ b/solution.py
@@ -39,15 +39,28 @@
         quarters[i] = mine
 
 
+def pack_kernel(slots, out):
+    value = slots[...].astype(F32)
+    left = lax.broadcasted_iota(jnp.int32, (64, 128), 1) < 64
+    out[:64] = jnp.where(left, value[:64], pltpu.roll(value[64:], 64, 1)).astype(BF)
+    out[64:] = value.T[64:80].astype(BF)
+
+
 def update_kernel(core, message, state, table_out, accum_out, block):
     rows = state.shape[1]
     total = jnp.zeros((128, rows), F32)
-    step = 512
-    for start in range(0, message.shape[0], step):
-        part = message[start : start + step]
-        target = (part[:, 64:65].astype(F32) * 32.0 + part[:, 65:66].astype(F32)).astype(jnp.int32)
-        picks = (target == lax.broadcasted_iota(jnp.int32, (step, rows), 1)).astype(F32).astype(BF)
-        total += lax.dot_general(part, picks, (((0,), (0,)), ((), ())), preferred_element_type=F32)
+    left = lax.broadcasted_iota(jnp.int32, (1, 128), 1) < 64
+    row = lax.broadcasted_iota(jnp.int32, (rows, 128), 0).astype(F32)
+    for start in range(0, message.shape[0], 160):
+        values = [message[at : at + 64].astype(F32) for at in (start, start + 80)]
+        digits = [message[at : at + 16].astype(F32) for at in (start + 64, start + 144)]
+        one, two = (part[0:1] * 32.0 + part[1:2] for part in digits)
+        values = jnp.concatenate(values, axis=0)
+        values = jnp.concatenate([values, pltpu.roll(values, 64, 1)], axis=0).astype(BF)
+        first = jnp.where(left, one, pltpu.roll(two, 64, 1))
+        second = jnp.where(left, pltpu.roll(one, 64, 1), two)
+        picks = jnp.concatenate([(row == target).astype(F32).astype(BF) for target in (first, second)], axis=1)
+        total += lax.dot_general(values, picks, (((0,), (1,)), ((), ())), preferred_element_type=F32)
     grad = total[:64]
     accum_new = state[64:] + grad * grad
     table_new = state[:64] - 0.5 * grad * lax.rsqrt(accum_new)
@@ -97,7 +110,7 @@
             pooled[j, pl.ds(r, 1), :] = jnp.where(left, bag(2 * j, r), bag(2 * j + 1, r))
         return carry
 
-    lax.fori_loop(0, requests, look_up, 0, unroll=4)
+    lax.fori_loop(0, requests, look_up, 0, unroll=8)
     features = jnp.concatenate([pooled[j].astype(BF) for j in range(pairs)], axis=1)
     columns = [pl.ds(pl.multiple_of((part[0] ^ i) * width, width), width) for i in range(4)]
     offset = jnp.concatenate([bias[:, at] for at in columns], axis=1)
@@ -141,7 +154,15 @@
     got = lax.all_to_all(message.reshape(32, 4, 128), ("x", "z"), 0, 0, tiled=True)
     got, quarters, state = lax.optimization_barrier((got, quarters, state))
     first = lax.all_to_all(quarters, ("x", "z"), 0, 0, tiled=True).reshape(1536, 256)
-    slots = lax.all_gather(got, ("y", "c"), axis=0, tiled=True).reshape(2048, 128)
+    packed = pl.pallas_call(
+        pack_kernel,
+        out_shape=jax.ShapeDtypeStruct((80, 128), BF),
+        in_specs=[VMEM],
+        out_specs=VMEM,
+        compiler_params=SMALL,
+        name="pack",
+    )(got.reshape(128, 128))
+    slots = lax.all_gather(packed, ("y", "c"), axis=0, tiled=True)
     table_out, accum_out, block = pl.pallas_call(
         update_kernel,
         out_shape=(

time: 127 us -> 127 us (level)
  no operation moved by 1% of the time
where the time goes in v5:
time: 127 us; the launch traced here: 126 us
  blocking collectives  44.7 us (35%)
  starting transfers between devices  39.3 us (31%)
  waiting for transfers between devices  17.7 us (14%)
  Pallas kernels  15.8 us (12%)
  local copies, waits for them, and re-layouts  6.75 us (5%)
    all_to_all x1, blocking collectives, per_device(): column = lax.all_to_all(block, 'z', 0, 0, tiled=True).reshape(2048, 128)  24.3 us
    all_gather x1, blocking collectives, per_device(): slots = lax.all_gather(packed, ('y', 'c'), axis=0, tiled=True)  20.4 us
    ppermute x6, starting transfers between devices, shift(): lax.ppermute(value, axis, [(i, (i + by) % size) for i in range(size)])  17.6 us
    all_to_all x1, starting transfers between devices, per_device(): lax.all_to_all(message.reshape(32, 4, 128), ('x', 'z'), 0, 0, tiled=True)  13.7 us
    pallas_call x1, Pallas kernels, per_device(): pl.pallas_call(score_kernel, out_shape=jax.ShapeDtypeStruct((256,), F32),...  11.4 us
    ppermute x6, waiting for transfers between devices, shift(): lax.ppermute(value, axis, [(i, (i + by) % size) for i in range(size)])  9.79 us
    all_to_all x1, waiting for transfers between devices, per_device(): lax.all_to_all(message.reshape(32, 4, 128), ('x', 'z'), 0, 0, tiled=True)  7.69 us
    unnamed x14, local copies, waits for them, and re-layouts  4.27 us
  transfers between devices with their start and end apart: 9, of which 4 were waited for; matrix products, arithmetic and copies ran while one was open for 5% of the time, Pallas kernels for 2%

profile of v5, /device:TPU:1, one launch (start us, length us, event | category | flops | bytes accessed | tf_op | source)
XLA Modules:
  0.0 126.2 jit_solution(17121798811733370803)
XLA Ops:
  0.6 1.9 %message.1 = (bf16[128,128]{1,0:T(8,128)(2,1)}, bf16[32,48,256]{2,1,0:T(8,128)(2,1)}) custom-call(s32[1]{0:T(128)} %bitcast.1.part, f32[64,128]{1,0:T(8,128)} %bitcast.51, s32[1,128]{1,0:T(1,128)} %bitcast.53, s32[1,32]{1,0:T(1,128)} %bitcast.54, bf16[48,1024]{1,0:T(8,128)(2,1)} %weights.1), custom_call_target="tpu_custom_call" | custom-call | tf_op jit(solution)/shard_map/message/pallas_call | solution.py:147
  2.5 13.7 %all-to-all-start = ((bf16[32,4,128]{2,1,0:T(4,128)(2,1)}), bf16[32,4,128]{2,1,0:T(4,128)(2,1)S(1)}, u32[]{:S(2)}, u32[]{:S(2)}) async-start(bf16[32,4,128]{2,1,0:T(4,128)(2,1)} %bitcast.50), calls=%async_computation | async-start | bytes 65536 | tf_op jit(solution)/shard_map/all_to_all | solution.py:154
  16.3 1.1 pad_maximum_fusion.state
  17.3 7.7 %all-to-all-done = bf16[32,4,128]{2,1,0:T(4,128)(2,1)S(1)} async-done(((bf16[32,4,128]{2,1,0:T(4,128)(2,1)}), bf16[32,4,128]{2,1,0:T(4,128)(2,1)S(1)}, u32[]{:S(2)}, u32[]{:S(2)}) %all-to-all-start) | async-done | bytes 32800 | tf_op jit(solution)/shard_map/all_to_all | solution.py:154
  25.0 3.9 %all-to-all-start.1 = ((bf16[32,48,256]{2,1,0:T(8,128)(2,1)}), bf16[32,48,256]{2,1,0:T(8,128)(2,1)S(1)}, u32[]{:S(2)}, u32[]{:S(2)}) async-start(bf16[32,48,256]{2,1,0:T(8,128)(2,1)} %get-tuple-element.24), calls=%async_computation.1 | async-start | bytes 1572864 | tf_op jit(solution)/shard_map/all_to_all | solution.py:156
  28.9 0.1 pack.1
  29.0 20.4 %all_gather.3.message = bf16[1280,128]{1,0:T(8,128)(2,1)S(1)} all-gather(bf16[80,128]{1,0:T(8,128)(2,1)S(1)} %pack.1), channel_id=1, replica_groups=mesh['y'=8,'c'=2,'x'=4,'z'=8] {'y','c'}, dimensions={0}, use_global_device_ids=true | all-gather | bytes 348160 | tf_op jit(solution)/shard_map/all_gather | solution.py:165
  49.5 2.4 %update.1 = (f32[64,1024]{1,0:T(8,128)}, f32[64,1024]{1,0:T(8,128)}, bf16[8,256,128]{2,1,0:T(8,128)(2,1)S(1)}) custom-call(s32[1]{0:T(128)} %bitcast.core, bf16[1280,128]{1,0:T(8,128)(2,1)S(1)} %all_gather.3.message, f32[128,1024]{1,0:T(8,128)S(1)} %pad_maximum_fusion.state), custom_call_target="tpu_custom_call" | custom-call | tf_op jit(solution)/shard_map/update/pallas_call | solution.py:166
  51.8 0.0 all-to-all-done.1
  51.8 24.3 %all_to_all.20 = bf16[8,256,128]{2,1,0:T(8,128)(2,1)S(1)} all-to-all(bf16[8,256,128]{2,1,0:T(8,128)(2,1)S(1)} %get-tuple-element.25), channel_id=1, replica_groups=mesh['y'=8,'c'=2,'x'=4,'z'=8] {'z'}, dimensions={0} | all-to-all | bytes 1048576 | tf_op jit(solution)/shard_map/all_to_all | solution.py:179
  76.1 1.6 %broadcast_in_dim.35 = bf16[4,2048,128]{2,1,0:T(8,128)(2,1)} broadcast(bf16[2048,128]{1,0:T(8,128)(2,1)S(1)} %bitcast.47), dimensions={1,2} | broadcast | bytes 2621440 | tf_op jit(solution)/shard_map/broadcast_in_dim | solution.py:183
  77.7 4.1 %all-to-all-start.3 = ((bf16[4,2048,128]{2,1,0:T(8,128)(2,1)}), bf16[4,2048,128]{2,1,0:T(8,128)(2,1)S(1)}, u32[]{:S(2)}, u32[]{:S(2)}) async-start(bf16[4,2048,128]{2,1,0:T(8,128)(2,1)} %broadcast_in_dim.35), calls=%async_computation.3 | async-start | bytes 4194304 | tf_op jit(solution)/shard_map/all_to_all | solution.py:184
  81.8 2.7 %collective-permute-start.2 = (bf16[1536,256]{1,0:T(8,128)(2,1)S(1)}, bf16[1536,256]{1,0:T(8,128)(2,1)S(1)}, u32[]{:S(2)}, u32[]{:S(2)}) collective-permute-start(bf16[1536,256]{1,0:T(8,128)(2,1)S(1)} %bitcast.44), channel_id=1, source_target_pairs={{0,32},{32,0},{1,33},{33,1},{2,34},{34,2},{3,35},{35,3},{4,36},{36... | collective-permute-start | bytes 2359304 | tf_op jit(solution)/shard_map/ppermute | solution.py:129
  84.6 0.1 fusion.3
  84.6 1.9 %collective-permute-start = (bf16[768,256]{1,0:T(8,128)(2,1)S(1)}, bf16[768,256]{1,0:T(8,128)(2,1)S(1)}, u32[]{:S(2)}, u32[]{:S(2)}) collective-permute-start(bf16[768,256]{1,0:T(8,128)(2,1)S(1)} %get-tuple-element.32), channel_id=1, source_target_pairs={{0,64},{64,128},{128,192},{192,256},{256,320},{320,384},{384,448},... | collective-permute-start | bytes 1179656 | tf_op jit(solution)/shard_map/ppermute | solution.py:129
  86.5 0.0 copy-start.1
  86.6 0.0 copy-start.2
  86.6 0.0 copy-start.3
  86.6 0.0 copy-start
  86.6 4.7 %collective-permute-start.1 = (bf16[768,256]{1,0:T(8,128)(2,1)S(1)}, bf16[768,256]{1,0:T(8,128)(2,1)S(1)}, u32[]{:S(2)}, u32[]{:S(2)}) collective-permute-start(bf16[768,256]{1,0:T(8,128)(2,1)S(1)} %get-tuple-element.31), channel_id=1, source_target_pairs={{0,448},{64,0},{128,64},{192,128},{256,192},{320,256},{384,320},{4... | collective-permute-start | bytes 1179656 | tf_op jit(solution)/shard_map/ppermute | solution.py:129
  91.3 0.9 constant_dynamic-update-slice_fusion.5
  92.2 6.2 %collective-permute-done = bf16[768,256]{1,0:T(8,128)(2,1)S(1)} collective-permute-done((bf16[768,256]{1,0:T(8,128)(2,1)S(1)}, bf16[768,256]{1,0:T(8,128)(2,1)S(1)}, u32[]{:S(2)}, u32[]{:S(2)}) %collective-permute-start) | collective-permute-done | bytes 393248 | tf_op jit(solution)/shard_map/ppermute | solution.py:129
  98.5 2.7 %collective-permute-start.3 = (bf16[768,256]{1,0:T(8,128)(2,1)S(1)}, bf16[768,256]{1,0:T(8,128)(2,1)S(1)}, u32[]{:S(2)}, u32[]{:S(2)}) collective-permute-start(bf16[768,256]{1,0:T(8,128)(2,1)S(1)} %collective-permute-done), channel_id=1, source_target_pairs={{0,32},{32,0},{1,33},{33,1},{2,34},{34,2},{3,35},{35,3},{4,36},{36... | collective-permute-start | bytes 1179656 | tf_op jit(solution)/shard_map/ppermute | solution.py:129
  101.2 0.8 constant_dynamic-update-slice_fusion.4
  101.9 0.0 collective-permute-done.1
  101.9 1.9 %collective-permute-start.4 = (bf16[768,256]{1,0:T(8,128)(2,1)S(1)}, bf16[768,256]{1,0:T(8,128)(2,1)S(1)}, u32[]{:S(2)}, u32[]{:S(2)}) collective-permute-start(bf16[768,256]{1,0:T(8,128)(2,1)S(1)} %collective-permute-done.1), channel_id=1, source_target_pairs={{0,32},{32,0},{1,33},{33,1},{2,34},{34,2},{3,35},{35,3},{4,36},{36... | collective-permute-start | bytes 1179656 | tf_op jit(solution)/shard_map/ppermute | solution.py:129
  103.9 0.8 constant_dynamic-update-slice_fusion.3
  104.6 0.0 collective-permute-done.2
  104.6 0.9 constant_dynamic-update-slice_fusion.2
  105.6 0.0 collective-permute-done.3
  105.6 0.8 constant_dynamic-update-slice_fusion.1
  106.4 0.0 collective-permute-done.4
  106.4 0.8 constant_dynamic-update-slice_fusion.weights_in
  107.2 0.2 all-to-all-done.3
  107.4 3.6 %collective-permute-start.5 = (bf16[8192,128]{1,0:T(8,128)(2,1)S(1)}, bf16[8192,128]{1,0:T(8,128)(2,1)S(1)}, u32[]{:S(2)}, u32[]{:S(2)}) collective-permute-start(bf16[8192,128]{1,0:T(8,128)(2,1)S(1)} %bitcast.39), channel_id=1, source_target_pairs={{0,32},{32,0},{1,33},{33,1},{2,34},{34,2},{3,35},{35,3},{4,36},{36... | collective-permute-start | bytes 6291464 | tf_op jit(solution)/shard_map/ppermute | solution.py:129
  111.0 0.0 copy-done.1
  111.0 0.0 copy-done.2
  111.0 0.1 fusion
  111.2 0.0 copy-done.3
  111.2 3.6 %collective-permute-done.5.other = bf16[8192,128]{1,0:T(8,128)(2,1)S(1)} collective-permute-done((bf16[8192,128]{1,0:T(8,128)(2,1)S(1)}, bf16[8192,128]{1,0:T(8,128)(2,1)S(1)}, u32[]{:S(2)}, u32[]{:S(2)}) %collective-permute-start.5) | collective-permute-done | bytes 2097184 | tf_op jit(solution)/shard_map/ppermute | solution.py:129
  114.8 0.0 copy-done
  114.8 11.4 %score.1 = f32[256]{0:T(256)} custom-call(s32[1]{0:T(128)} %bitcast.1.part, s32[12288]{0:T(1024)S(1)} %bitcast.41, bf16[8192,128]{1,0:T(8,128)(2,1)S(1)} %bitcast.40, bf16[8192,128]{1,0:T(8,128)(2,1)S(1)} %collective-permute-done.5.other, bf16[6144,256]{1,0:T(8,128)(2,1)} %constant_dynamic-update-slice_fusion.weights_in, f32[1,1024]{1,0:T(1,128)S(1)} %bitcast.43, ...), custom_call_target="tpu_custom_call" | custom-call | tf_op jit(solution)/shard_map/score/pallas_call | solution.py:196
  (2 shorter events, 0.0 us)
Async XLA Ops:
  2.5 22.5 %all-to-all-start = ((bf16[32,4,128]{2,1,0:T(4,128)(2,1)}), bf16[32,4,128]{2,1,0:T(4,128)(2,1)S(1)}, u32[]{:S(2)}, u32[]{:S(2)}) async-start(bf16[32,4,128]{2,1,0:T(4,128)(2,1)} %bitcast.50), calls=%async_computation | async-start | bytes 65536 | tf_op jit(solution)/shard_map/all_to_all | solution.py:154
  25.0 26.8 %all-to-all-start.1 = ((bf16[32,48,256]{2,1,0:T(8,128)(2,1)}), bf16[32,48,256]{2,1,0:T(8,128)(2,1)S(1)}, u32[]{:S(2)}, u32[]{:S(2)}) async-start(bf16[32,48,256]{2,1,0:T(8,128)(2,1)} %get-tuple-element.24), calls=%async_computation.1 | async-start | bytes 1572864 | tf_op jit(solution)/shard_map/all_to_all | solution.py:156
  77.7 29.6 %all-to-all-start.3 = ((bf16[4,2048,128]{2,1,0:T(8,128)(2,1)}), bf16[4,2048,128]{2,1,0:T(8,128)(2,1)S(1)}, u32[]{:S(2)}, u32[]{:S(2)}) async-start(bf16[4,2048,128]{2,1,0:T(8,128)(2,1)} %broadcast_in_dim.35), calls=%async_computation.3 | async-start | bytes 4194304 | tf_op jit(solution)/shard_map/all_to_all | solution.py:184
  81.8 22.8 %collective-permute-start.2 = (bf16[1536,256]{1,0:T(8,128)(2,1)S(1)}, bf16[1536,256]{1,0:T(8,128)(2,1)S(1)}, u32[]{:S(2)}, u32[]{:S(2)}) collective-permute-start(bf16[1536,256]{1,0:T(8,128)(2,1)S(1)} %bitcast.44), channel_id=1, source_target_pairs={{0,32},{32,0},{1,33},{33,1},{2,34},{34,2},{3,35},{35,3},{4,36},{36... | collective-permute-start | bytes 2359304 | tf_op jit(solution)/shard_map/ppermute | solution.py:129
  84.6 13.8 %collective-permute-start = (bf16[768,256]{1,0:T(8,128)(2,1)S(1)}, bf16[768,256]{1,0:T(8,128)(2,1)S(1)}, u32[]{:S(2)}, u32[]{:S(2)}) collective-permute-start(bf16[768,256]{1,0:T(8,128)(2,1)S(1)} %get-tuple-element.32), channel_id=1, source_target_pairs={{0,64},{64,128},{128,192},{192,256},{256,320},{320,384},{384,448},... | collective-permute-start | bytes 1179656 | tf_op jit(solution)/shard_map/ppermute | solution.py:129
  86.5 24.5 %copy-start.1 = (s32[256,24,2]{0,2,1:T(2,128)S(1)}, s32[256,24,2]{0,2,1:T(2,128)}, u32[]{:S(2)}) copy-start(s32[256,24,2]{0,2,1:T(2,128)} %param.15) | copy-start | bytes 147460
  86.6 24.5 %copy-start.2 = (s32[256,24]{0,1:T(8,128)S(1)}, s32[256,24]{0,1:T(8,128)}, u32[]{:S(2)}) copy-start(s32[256,24]{0,1:T(8,128)} %param.16) | copy-start | bytes 73732
  86.6 24.6 %copy-start.3 = (bf16[1024]{0:T(1024)(128)(2,1)S(1)}, bf16[1024]{0:T(1024)(128)(2,1)}, u32[]{:S(2)}) copy-start(bf16[1024]{0:T(1024)(128)(2,1)} %param.19) | copy-start | bytes 6148
  86.6 28.2 %copy-start = (f32[1024]{0:T(1024)S(1)}, f32[1024]{0:T(1024)}, u32[]{:S(2)}) copy-start(f32[1024]{0:T(1024)} %param.18) | copy-start | bytes 12292
  86.6 15.4 %collective-permute-start.1 = (bf16[768,256]{1,0:T(8,128)(2,1)S(1)}, bf16[768,256]{1,0:T(8,128)(2,1)S(1)}, u32[]{:S(2)}, u32[]{:S(2)}) collective-permute-start(bf16[768,256]{1,0:T(8,128)(2,1)S(1)} %get-tuple-element.31), channel_id=1, source_target_pairs={{0,448},{64,0},{128,64},{192,128},{256,192},{320,256},{384,320},{4... | collective-permute-start | bytes 1179656 | tf_op jit(solution)/shard_map/ppermute | solution.py:129
  98.5 7.1 %collective-permute-start.3 = (bf16[768,256]{1,0:T(8,128)(2,1)S(1)}, bf16[768,256]{1,0:T(8,128)(2,1)S(1)}, u32[]{:S(2)}, u32[]{:S(2)}) collective-permute-start(bf16[768,256]{1,0:T(8,128)(2,1)S(1)} %collective-permute-done), channel_id=1, source_target_pairs={{0,32},{32,0},{1,33},{33,1},{2,34},{34,2},{3,35},{35,3},{4,36},{36... | collective-permute-start | bytes 1179656 | tf_op jit(solution)/shard_map/ppermute | solution.py:129
  101.9 4.4 %collective-permute-start.4 = (bf16[768,256]{1,0:T(8,128)(2,1)S(1)}, bf16[768,256]{1,0:T(8,128)(2,1)S(1)}, u32[]{:S(2)}, u32[]{:S(2)}) collective-permute-start(bf16[768,256]{1,0:T(8,128)(2,1)S(1)} %collective-permute-done.1), channel_id=1, source_target_pairs={{0,32},{32,0},{1,33},{33,1},{2,34},{34,2},{3,35},{35,3},{4,36},{36... | collective-permute-start | bytes 1179656 | tf_op jit(solution)/shard_map/ppermute | solution.py:129
  107.4 7.4 %collective-permute-start.5 = (bf16[8192,128]{1,0:T(8,128)(2,1)S(1)}, bf16[8192,128]{1,0:T(8,128)(2,1)S(1)}, u32[]{:S(2)}, u32[]{:S(2)}) collective-permute-start(bf16[8192,128]{1,0:T(8,128)(2,1)S(1)} %bitcast.39), channel_id=1, source_target_pairs={{0,32},{32,0},{1,33},{33,1},{2,34},{34,2},{3,35},{35,3},{4,36},{36... | collective-permute-start | bytes 6291464 | tf_op jit(solution)/shard_map/ppermute | solution.py:129

commit v6 on v5

--- a/solution.py
+++ b/solution.py
@@ -110,7 +110,7 @@
             pooled[j, pl.ds(r, 1), :] = jnp.where(left, bag(2 * j, r), bag(2 * j + 1, r))
         return carry
 
-    lax.fori_loop(0, requests, look_up, 0, unroll=8)
+    lax.fori_loop(0, requests, look_up, 0, unroll=16)
     features = jnp.concatenate([pooled[j].astype(BF) for j in range(pairs)], axis=1)
     columns = [pl.ds(pl.multiple_of((part[0] ^ i) * width, width), width) for i in range(4)]
     offset = jnp.concatenate([bias[:, at] for at in columns], axis=1)

time: 127 us -> 127 us (level)
  no operation moved by 1% of the time
where the time goes in v6:
time: 127 us; the launch traced here: 126 us
  blocking collectives  44.7 us (35%)
  starting transfers between devices  39.3 us (31%)
  waiting for transfers between devices  17.7 us (14%)
  Pallas kernels  15.7 us (12%)
  local copies, waits for them, and re-layouts  6.75 us (5%)
    all_to_all x1, blocking collectives, per_device(): column = lax.all_to_all(block, 'z', 0, 0, tiled=True).reshape(2048, 128)  24.3 us
    all_gather x1, blocking collectives, per_device(): slots = lax.all_gather(packed, ('y', 'c'), axis=0, tiled=True)  20.4 us
    ppermute x6, starting transfers between devices, shift(): lax.ppermute(value, axis, [(i, (i + by) % size) for i in range(size)])  17.6 us
    all_to_all x1, starting transfers between devices, per_device(): lax.all_to_all(message.reshape(32, 4, 128), ('x', 'z'), 0, 0, tiled=True)  13.7 us
    pallas_call x1, Pallas kernels, per_device(): pl.pallas_call(score_kernel, out_shape=jax.ShapeDtypeStruct((256,), F32),...  11.3 us
    ppermute x6, waiting for transfers between devices, shift(): lax.ppermute(value, axis, [(i, (i + by) % size) for i in range(size)])  9.79 us
    all_to_all x1, waiting for transfers between devices, per_device(): lax.all_to_all(message.reshape(32, 4, 128), ('x', 'z'), 0, 0, tiled=True)  7.69 us
    unnamed x14, local copies, waits for them, and re-layouts  4.27 us
  transfers between devices with their start and end apart: 9, of which 4 were waited for; matrix products, arithmetic and copies ran while one was open for 5% of the time, Pallas kernels for 2%

profile of v6, /device:TPU:1, one launch (start us, length us, event | category | flops | bytes accessed | tf_op | source)
XLA Modules:
  0.0 126.1 jit_solution(18104143622632857569)
XLA Ops:
  0.6 1.9 %message.1 = (bf16[128,128]{1,0:T(8,128)(2,1)}, bf16[32,48,256]{2,1,0:T(8,128)(2,1)}) custom-call(s32[1]{0:T(128)} %bitcast.1.part, f32[64,128]{1,0:T(8,128)} %bitcast.51, s32[1,128]{1,0:T(1,128)} %bitcast.53, s32[1,32]{1,0:T(1,128)} %bitcast.54, bf16[48,1024]{1,0:T(8,128)(2,1)} %weights.1), custom_call_target="tpu_custom_call" | custom-call | tf_op jit(solution)/shard_map/message/pallas_call | solution.py:147
  2.5 13.7 %all-to-all-start = ((bf16[32,4,128]{2,1,0:T(4,128)(2,1)}), bf16[32,4,128]{2,1,0:T(4,128)(2,1)S(1)}, u32[]{:S(2)}, u32[]{:S(2)}) async-start(bf16[32,4,128]{2,1,0:T(4,128)(2,1)} %bitcast.50), calls=%async_computation | async-start | bytes 65536 | tf_op jit(solution)/shard_map/all_to_all | solution.py:154
  16.3 1.1 pad_maximum_fusion.state
  17.3 7.7 %all-to-all-done = bf16[32,4,128]{2,1,0:T(4,128)(2,1)S(1)} async-done(((bf16[32,4,128]{2,1,0:T(4,128)(2,1)}), bf16[32,4,128]{2,1,0:T(4,128)(2,1)S(1)}, u32[]{:S(2)}, u32[]{:S(2)}) %all-to-all-start) | async-done | bytes 32800 | tf_op jit(solution)/shard_map/all_to_all | solution.py:154
  25.0 3.9 %all-to-all-start.1 = ((bf16[32,48,256]{2,1,0:T(8,128)(2,1)}), bf16[32,48,256]{2,1,0:T(8,128)(2,1)S(1)}, u32[]{:S(2)}, u32[]{:S(2)}) async-start(bf16[32,48,256]{2,1,0:T(8,128)(2,1)} %get-tuple-element.24), calls=%async_computation.1 | async-start | bytes 1572864 | tf_op jit(solution)/shard_map/all_to_all | solution.py:156
  28.9 0.1 pack.1
  29.0 20.4 %all_gather.3.message = bf16[1280,128]{1,0:T(8,128)(2,1)S(1)} all-gather(bf16[80,128]{1,0:T(8,128)(2,1)S(1)} %pack.1), channel_id=1, replica_groups=mesh['y'=8,'c'=2,'x'=4,'z'=8] {'y','c'}, dimensions={0}, use_global_device_ids=true | all-gather | bytes 348160 | tf_op jit(solution)/shard_map/all_gather | solution.py:165
  49.5 2.4 %update.1 = (f32[64,1024]{1,0:T(8,128)}, f32[64,1024]{1,0:T(8,128)}, bf16[8,256,128]{2,1,0:T(8,128)(2,1)S(1)}) custom-call(s32[1]{0:T(128)} %bitcast.core, bf16[1280,128]{1,0:T(8,128)(2,1)S(1)} %all_gather.3.message, f32[128,1024]{1,0:T(8,128)S(1)} %pad_maximum_fusion.state), custom_call_target="tpu_custom_call" | custom-call | tf_op jit(solution)/shard_map/update/pallas_call | solution.py:166
  51.8 0.0 all-to-all-done.1
  51.8 24.3 %all_to_all.20 = bf16[8,256,128]{2,1,0:T(8,128)(2,1)S(1)} all-to-all(bf16[8,256,128]{2,1,0:T(8,128)(2,1)S(1)} %get-tuple-element.25), channel_id=1, replica_groups=mesh['y'=8,'c'=2,'x'=4,'z'=8] {'z'}, dimensions={0} | all-to-all | bytes 1048576 | tf_op jit(solution)/shard_map/all_to_all | solution.py:179
  76.1 1.6 %broadcast_in_dim.35 = bf16[4,2048,128]{2,1,0:T(8,128)(2,1)} broadcast(bf16[2048,128]{1,0:T(8,128)(2,1)S(1)} %bitcast.47), dimensions={1,2} | broadcast | bytes 2621440 | tf_op jit(solution)/shard_map/broadcast_in_dim | solution.py:183
  77.7 4.1 %all-to-all-start.3 = ((bf16[4,2048,128]{2,1,0:T(8,128)(2,1)}), bf16[4,2048,128]{2,1,0:T(8,128)(2,1)S(1)}, u32[]{:S(2)}, u32[]{:S(2)}) async-start(bf16[4,2048,128]{2,1,0:T(8,128)(2,1)} %broadcast_in_dim.35), calls=%async_computation.3 | async-start | bytes 4194304 | tf_op jit(solution)/shard_map/all_to_all | solution.py:184
  81.8 2.7 %collective-permute-start.2 = (bf16[1536,256]{1,0:T(8,128)(2,1)S(1)}, bf16[1536,256]{1,0:T(8,128)(2,1)S(1)}, u32[]{:S(2)}, u32[]{:S(2)}) collective-permute-start(bf16[1536,256]{1,0:T(8,128)(2,1)S(1)} %bitcast.44), channel_id=1, source_target_pairs={{0,32},{32,0},{1,33},{33,1},{2,34},{34,2},{3,35},{35,3},{4,36},{36... | collective-permute-start | bytes 2359304 | tf_op jit(solution)/shard_map/ppermute | solution.py:129
  84.6 0.1 fusion.3
  84.6 1.9 %collective-permute-start = (bf16[768,256]{1,0:T(8,128)(2,1)S(1)}, bf16[768,256]{1,0:T(8,128)(2,1)S(1)}, u32[]{:S(2)}, u32[]{:S(2)}) collective-permute-start(bf16[768,256]{1,0:T(8,128)(2,1)S(1)} %get-tuple-element.32), channel_id=1, source_target_pairs={{0,64},{64,128},{128,192},{192,256},{256,320},{320,384},{384,448},... | collective-permute-start | bytes 1179656 | tf_op jit(solution)/shard_map/ppermute | solution.py:129
  86.5 0.0 copy-start.1
  86.6 0.0 copy-start.2
  86.6 0.0 copy-start.3
  86.6 0.0 copy-start
  86.6 4.7 %collective-permute-start.1 = (bf16[768,256]{1,0:T(8,128)(2,1)S(1)}, bf16[768,256]{1,0:T(8,128)(2,1)S(1)}, u32[]{:S(2)}, u32[]{:S(2)}) collective-permute-start(bf16[768,256]{1,0:T(8,128)(2,1)S(1)} %get-tuple-element.31), channel_id=1, source_target_pairs={{0,448},{64,0},{128,64},{192,128},{256,192},{320,256},{384,320},{4... | collective-permute-start | bytes 1179656 | tf_op jit(solution)/shard_map/ppermute | solution.py:129
  91.3 0.9 constant_dynamic-update-slice_fusion.5
  92.2 6.2 %collective-permute-done = bf16[768,256]{1,0:T(8,128)(2,1)S(1)} collective-permute-done((bf16[768,256]{1,0:T(8,128)(2,1)S(1)}, bf16[768,256]{1,0:T(8,128)(2,1)S(1)}, u32[]{:S(2)}, u32[]{:S(2)}) %collective-permute-start) | collective-permute-done | bytes 393248 | tf_op jit(solution)/shard_map/ppermute | solution.py:129
  98.5 2.7 %collective-permute-start.3 = (bf16[768,256]{1,0:T(8,128)(2,1)S(1)}, bf16[768,256]{1,0:T(8,128)(2,1)S(1)}, u32[]{:S(2)}, u32[]{:S(2)}) collective-permute-start(bf16[768,256]{1,0:T(8,128)(2,1)S(1)} %collective-permute-done), channel_id=1, source_target_pairs={{0,32},{32,0},{1,33},{33,1},{2,34},{34,2},{3,35},{35,3},{4,36},{36... | collective-permute-start | bytes 1179656 | tf_op jit(solution)/shard_map/ppermute | solution.py:129
  101.2 0.8 constant_dynamic-update-slice_fusion.4
  101.9 0.0 collective-permute-done.1
  101.9 1.9 %collective-permute-start.4 = (bf16[768,256]{1,0:T(8,128)(2,1)S(1)}, bf16[768,256]{1,0:T(8,128)(2,1)S(1)}, u32[]{:S(2)}, u32[]{:S(2)}) collective-permute-start(bf16[768,256]{1,0:T(8,128)(2,1)S(1)} %collective-permute-done.1), channel_id=1, source_target_pairs={{0,32},{32,0},{1,33},{33,1},{2,34},{34,2},{3,35},{35,3},{4,36},{36... | collective-permute-start | bytes 1179656 | tf_op jit(solution)/shard_map/ppermute | solution.py:129
  103.9 0.8 constant_dynamic-update-slice_fusion.3
  104.6 0.0 collective-permute-done.2
  104.6 0.9 constant_dynamic-update-slice_fusion.2
  105.6 0.0 collective-permute-done.3
  105.6 0.8 constant_dynamic-update-slice_fusion.1
  106.4 0.0 collective-permute-done.4
  106.4 0.8 constant_dynamic-update-slice_fusion.weights_in
  107.2 0.2 all-to-all-done.3
  107.4 3.6 %collective-permute-start.5 = (bf16[8192,128]{1,0:T(8,128)(2,1)S(1)}, bf16[8192,128]{1,0:T(8,128)(2,1)S(1)}, u32[]{:S(2)}, u32[]{:S(2)}) collective-permute-start(bf16[8192,128]{1,0:T(8,128)(2,1)S(1)} %bitcast.39), channel_id=1, source_target_pairs={{0,32},{32,0},{1,33},{33,1},{2,34},{34,2},{3,35},{35,3},{4,36},{36... | collective-permute-start | bytes 6291464 | tf_op jit(solution)/shard_map/ppermute | solution.py:129
  111.0 0.0 copy-done.1
  111.0 0.0 copy-done.2
  111.0 0.1 fusion
  111.2 0.0 copy-done.3
  111.2 3.6 %collective-permute-done.5.other = bf16[8192,128]{1,0:T(8,128)(2,1)S(1)} collective-permute-done((bf16[8192,128]{1,0:T(8,128)(2,1)S(1)}, bf16[8192,128]{1,0:T(8,128)(2,1)S(1)}, u32[]{:S(2)}, u32[]{:S(2)}) %collective-permute-start.5) | collective-permute-done | bytes 2097184 | tf_op jit(solution)/shard_map/ppermute | solution.py:129
  114.8 0.0 copy-done
  114.8 11.3 %score.1 = f32[256]{0:T(256)} custom-call(s32[1]{0:T(128)} %bitcast.1.part, s32[12288]{0:T(1024)S(1)} %bitcast.41, bf16[8192,128]{1,0:T(8,128)(2,1)S(1)} %bitcast.40, bf16[8192,128]{1,0:T(8,128)(2,1)S(1)} %collective-permute-done.5.other, bf16[6144,256]{1,0:T(8,128)(2,1)} %constant_dynamic-update-slice_fusion.weights_in, f32[1,1024]{1,0:T(1,128)S(1)} %bitcast.43, ...), custom_call_target="tpu_custom_call" | custom-call | tf_op jit(solution)/shard_map/score/pallas_call | solution.py:196
  (2 shorter events, 0.0 us)
Async XLA Ops:
  2.5 22.5 %all-to-all-start = ((bf16[32,4,128]{2,1,0:T(4,128)(2,1)}), bf16[32,4,128]{2,1,0:T(4,128)(2,1)S(1)}, u32[]{:S(2)}, u32[]{:S(2)}) async-start(bf16[32,4,128]{2,1,0:T(4,128)(2,1)} %bitcast.50), calls=%async_computation | async-start | bytes 65536 | tf_op jit(solution)/shard_map/all_to_all | solution.py:154
  25.0 26.8 %all-to-all-start.1 = ((bf16[32,48,256]{2,1,0:T(8,128)(2,1)}), bf16[32,48,256]{2,1,0:T(8,128)(2,1)S(1)}, u32[]{:S(2)}, u32[]{:S(2)}) async-start(bf16[32,48,256]{2,1,0:T(8,128)(2,1)} %get-tuple-element.24), calls=%async_computation.1 | async-start | bytes 1572864 | tf_op jit(solution)/shard_map/all_to_all | solution.py:156
  77.7 29.6 %all-to-all-start.3 = ((bf16[4,2048,128]{2,1,0:T(8,128)(2,1)}), bf16[4,2048,128]{2,1,0:T(8,128)(2,1)S(1)}, u32[]{:S(2)}, u32[]{:S(2)}) async-start(bf16[4,2048,128]{2,1,0:T(8,128)(2,1)} %broadcast_in_dim.35), calls=%async_computation.3 | async-start | bytes 4194304 | tf_op jit(solution)/shard_map/all_to_all | solution.py:184
  81.8 22.8 %collective-permute-start.2 = (bf16[1536,256]{1,0:T(8,128)(2,1)S(1)}, bf16[1536,256]{1,0:T(8,128)(2,1)S(1)}, u32[]{:S(2)}, u32[]{:S(2)}) collective-permute-start(bf16[1536,256]{1,0:T(8,128)(2,1)S(1)} %bitcast.44), channel_id=1, source_target_pairs={{0,32},{32,0},{1,33},{33,1},{2,34},{34,2},{3,35},{35,3},{4,36},{36... | collective-permute-start | bytes 2359304 | tf_op jit(solution)/shard_map/ppermute | solution.py:129
  84.6 13.8 %collective-permute-start = (bf16[768,256]{1,0:T(8,128)(2,1)S(1)}, bf16[768,256]{1,0:T(8,128)(2,1)S(1)}, u32[]{:S(2)}, u32[]{:S(2)}) collective-permute-start(bf16[768,256]{1,0:T(8,128)(2,1)S(1)} %get-tuple-element.32), channel_id=1, source_target_pairs={{0,64},{64,128},{128,192},{192,256},{256,320},{320,384},{384,448},... | collective-permute-start | bytes 1179656 | tf_op jit(solution)/shard_map/ppermute | solution.py:129
  86.5 24.5 %copy-start.1 = (s32[256,24,2]{0,2,1:T(2,128)S(1)}, s32[256,24,2]{0,2,1:T(2,128)}, u32[]{:S(2)}) copy-start(s32[256,24,2]{0,2,1:T(2,128)} %param.15) | copy-start | bytes 147460
  86.6 24.5 %copy-start.2 = (s32[256,24]{0,1:T(8,128)S(1)}, s32[256,24]{0,1:T(8,128)}, u32[]{:S(2)}) copy-start(s32[256,24]{0,1:T(8,128)} %param.16) | copy-start | bytes 73732
  86.6 24.6 %copy-start.3 = (bf16[1024]{0:T(1024)(128)(2,1)S(1)}, bf16[1024]{0:T(1024)(128)(2,1)}, u32[]{:S(2)}) copy-start(bf16[1024]{0:T(1024)(128)(2,1)} %param.19) | copy-start | bytes 6148
  86.6 28.2 %copy-start = (f32[1024]{0:T(1024)S(1)}, f32[1024]{0:T(1024)}, u32[]{:S(2)}) copy-start(f32[1024]{0:T(1024)} %param.18) | copy-start | bytes 12292
  86.6 15.4 %collective-permute-start.1 = (bf16[768,256]{1,0:T(8,128)(2,1)S(1)}, bf16[768,256]{1,0:T(8,128)(2,1)S(1)}, u32[]{:S(2)}, u32[]{:S(2)}) collective-permute-start(bf16[768,256]{1,0:T(8,128)(2,1)S(1)} %get-tuple-element.31), channel_id=1, source_target_pairs={{0,448},{64,0},{128,64},{192,128},{256,192},{320,256},{384,320},{4... | collective-permute-start | bytes 1179656 | tf_op jit(solution)/shard_map/ppermute | solution.py:129
  98.5 7.1 %collective-permute-start.3 = (bf16[768,256]{1,0:T(8,128)(2,1)S(1)}, bf16[768,256]{1,0:T(8,128)(2,1)S(1)}, u32[]{:S(2)}, u32[]{:S(2)}) collective-permute-start(bf16[768,256]{1,0:T(8,128)(2,1)S(1)} %collective-permute-done), channel_id=1, source_target_pairs={{0,32},{32,0},{1,33},{33,1},{2,34},{34,2},{3,35},{35,3},{4,36},{36... | collective-permute-start | bytes 1179656 | tf_op jit(solution)/shard_map/ppermute | solution.py:129
  101.9 4.4 %collective-permute-start.4 = (bf16[768,256]{1,0:T(8,128)(2,1)S(1)}, bf16[768,256]{1,0:T(8,128)(2,1)S(1)}, u32[]{:S(2)}, u32[]{:S(2)}) collective-permute-start(bf16[768,256]{1,0:T(8,128)(2,1)S(1)} %collective-permute-done.1), channel_id=1, source_target_pairs={{0,32},{32,0},{1,33},{33,1},{2,34},{34,2},{3,35},{35,3},{4,36},{36... | collective-permute-start | bytes 1179656 | tf_op jit(solution)/shard_map/ppermute | solution.py:129
  107.4 7.4 %collective-permute-start.5 = (bf16[8192,128]{1,0:T(8,128)(2,1)S(1)}, bf16[8192,128]{1,0:T(8,128)(2,1)S(1)}, u32[]{:S(2)}, u32[]{:S(2)}) collective-permute-start(bf16[8192,128]{1,0:T(8,128)(2,1)S(1)} %bitcast.39), channel_id=1, source_target_pairs={{0,32},{32,0},{1,33},{33,1},{2,34},{34,2},{3,35},{35,3},{4,36},{36... | collective-permute-start | bytes 6291464 | tf_op jit(solution)/shard_map/ppermute | solution.py:129
